TPU v7x, 128 devices: a whole 4x4x4 slice. The times are simulated.
128 devices in a mesh: bead: 8 (over z, core), gx: 4 (over y), gy: 4 (over x).
Axes of the slice: x: 4, y: 4, z: 4, core: 2. Of those that a mesh axis runs over, the one named last changes fastest.
Arguments:
- positions: float32 [32, 3, 16384], P('bead', None, ('gx', 'gy')), may hold values from 0 to 3
- momenta: float32 [32, 3, 16384], P('bead', None, ('gx', 'gy')), may hold values from -0.24 to 0.24
- types: int32 [16384], P(('gx', 'gy')), may hold values from 0 to 1
- ghost_rows: int32 [2048], P(('gx', 'gy')), may hold values from 0 to 1023
- neighbours: int32 [16, 16384], P(None, ('gx', 'gy')), may hold values from 0 to 2175
- counts: int32 [16384], P(('gx', 'gy')), may hold values from 8 to 16
- hardness: float32 [2], replicated, may hold values from 0.5 to 1
- chi_w1: float32 [2, 25, 30], replicated, may hold values from -1 to 1
- chi_w2: float32 [2, 25, 25], replicated, may hold values from -1.25 to 1.25
- chi_w3: float32 [2, 25], replicated, may hold values from -1.25 to 1.25
- en_w1: float32 [2, 25, 31], replicated, may hold values from -1 to 1
- en_w2: float32 [2, 25, 25], replicated, may hold values from -1.25 to 1.25
- en_w3: float32 [2, 25], replicated, may hold values from -1.25 to 1.25
Outputs:
- new_positions: float32 [32, 3, 16384], P('bead', None, ('gx', 'gy'))
- new_momenta: float32 [32, 3, 16384], P('bead', None, ('gx', 'gy'))
- charges: float32 [32, 16384], P('bead', ('gx', 'gy'))
- energies: float32 [32, 16384], P('bead', ('gx', 'gy'))
All inputs are finite; a program needn't handle non-finite values.
Results may differ from a plain program's by a relative error of at most 0.0003.
Values sent between devices are 32-bit elements; how exact they have to be, the bound alone decides.
A program may use at most 128 MiB of HBM per device.

v0:
```python
import math

import jax
import jax.numpy as jnp
from jax import lax
from jax.sharding import PartitionSpec as P

ITERS = 5


PRECISE = lax.Precision.HIGHEST
STEP = 0.5
CYCLE_FREQ = 40.0
CUTOFF = 4.0
HEAVY_MASS = 16.0
CHI_SCALE = 4.0
COUPLING_SCALE = 16.0


def with_halo(cells, sides, width):
    for axis, dim in sides:
        count = lax.axis_size(axis)
        head = lax.slice_in_dim(cells, 0, width, axis=dim)
        tail = lax.slice_in_dim(cells, cells.shape[dim] - width, cells.shape[dim], axis=dim)
        cells = jnp.concatenate(
            [
                lax.ppermute(tail, axis, [(i, (i + 1) % count) for i in range(count)]),
                cells,
                lax.ppermute(head, axis, [((i + 1) % count, i) for i in range(count)]),
            ],
            axis=dim,
        )
    return cells


def mode_tables(beads):
    row_ids = jnp.arange(beads, dtype=jnp.float32)[:, None]
    col_ids = jnp.arange(beads, dtype=jnp.int32)[None, :]
    angle = 2.0 * math.pi * row_ids * col_ids.astype(jnp.float32) / beads
    edge = (col_ids == 0) | (2 * col_ids == beads)
    scaled = math.sqrt(2.0 / beads)
    matrix = jnp.where(
        edge,
        jnp.cos(angle) / math.sqrt(beads),
        jnp.where(2 * col_ids < beads, scaled * jnp.cos(angle), scaled * jnp.sin(angle)),
    )
    frequency = 2.0 * CYCLE_FREQ * jnp.sin(math.pi * jnp.arange(beads, dtype=jnp.float32) / beads)
    return (matrix, frequency)


def rotate_modes(normal_modes, masses, frequency):
    top_freq = 2.0 * CYCLE_FREQ
    coord_part = normal_modes[:, 0]
    moment_part = normal_modes[:, 1]
    omega = frequency[:, None, None]
    cosine = jnp.cos(omega * STEP)
    sine_part = jnp.sin(omega * STEP)
    moving = omega > 0
    safe_omega = jnp.where(moving, omega, 1.0)
    drift_term = jnp.where(
        moving, top_freq * sine_part / (masses * safe_omega), top_freq * STEP / masses
    )
    restoring = -(masses * omega / top_freq) * sine_part
    return jnp.stack(
        [
            cosine * coord_part + drift_term * moment_part,
            restoring * coord_part + cosine * moment_part,
        ],
        1,
    )


def radial_terms(dist_sq, heavy_w, light_w, half):
    heavy_rows = []
    light_rows = []
    for slot_index in range(half):
        decay_rate = 0.2 * 20.0 ** (slot_index / (half - 1))
        falloff = jnp.exp(-decay_rate * dist_sq)
        heavy_rows.append(jnp.sum(heavy_w * falloff, axis=-2))
        light_rows.append(jnp.sum(light_w * falloff, axis=-2))
    return jnp.log1p(jnp.stack(heavy_rows + light_rows, axis=-2))


def network(features, first_w, second_w, third_w, heavy):
    results = []
    for element in range(2):
        hidden = jnp.tanh(
            jnp.einsum("hs,...sa->...ha", first_w[element], features, precision=PRECISE)
        )
        hidden = jnp.tanh(
            jnp.einsum("hk,...ka->...ha", second_w[element], hidden, precision=PRECISE)
        )
        results.append(jnp.einsum("h,...ha->...a", third_w[element], hidden, precision=PRECISE))
    return jnp.where(heavy, results[0], results[1])


def unfold(beside_all):
    layers = beside_all.shape[2]
    width = beside_all.shape[3]
    return jnp.transpose(beside_all.reshape(9, layers, width), (1, 0, 2)).reshape(layers, 9 * width)


def spread_back(terms, neighbours, ghost_rows):
    leading = terms.shape[:-2]
    atoms = terms.shape[-1]
    ghost_count = ghost_rows.shape[0]
    flat = terms.reshape((-1,) + terms.shape[-2:])
    layers = flat.shape[0]
    table = jnp.zeros((layers, atoms + 9 * ghost_count), jnp.float32).at[:, neighbours].add(flat)
    blocks = table[:, atoms:].reshape(layers, 3, 3, ghost_count)
    beside_all = with_halo(blocks.reshape(layers, 9, 1, 1, ghost_count), (("gx", 2), ("gy", 3)), 1)
    received = beside_all[:, 8, 0, 0]
    for first_pick in range(3):
        for second_pick in range(3):
            if first_pick + second_pick > 0:
                received = (
                    received
                    + beside_all[:, 8 - 3 * first_pick - second_pick, first_pick, second_pick]
                )
    own = table[:, :atoms].at[:, ghost_rows].add(received)
    return own.reshape(leading + (atoms,))


def residual_sum(residual):
    return lax.psum(jnp.sum(residual * residual, -1), ("gx", "gy"))[..., None]


def on_device(
    positions,
    momenta,
    types,
    ghost_rows,
    neighbours,
    counts,
    hardness,
    chi_w1,
    chi_w2,
    chi_w3,
    en_w1,
    en_w2,
    en_w3,
):
    per_dev = positions.shape[0]
    groups = lax.axis_size("bead")
    beads = per_dev * groups
    matrix, frequency = mode_tables(beads)
    heavy_atoms = types == 0
    masses = jnp.where(heavy_atoms, HEAVY_MASS, 1.0)
    phase_space = jnp.stack([positions, momenta], 1)
    gathered = lax.all_gather(phase_space, "bead", axis=0, tiled=True)
    own_rows = lax.dynamic_slice_in_dim(matrix, lax.axis_index("bead") * per_dev, per_dev, 0)
    normal_modes = jnp.einsum("jk,jsca->ksca", matrix, gathered, precision=PRECISE)
    advanced = jnp.einsum(
        "jk,ksca->jsca", own_rows, rotate_modes(normal_modes, masses, frequency), precision=PRECISE
    )
    new_positions = advanced[:, 0]
    new_momenta = advanced[:, 1]
    ghost_count = ghost_rows.shape[0]
    heavy_f = heavy_atoms.astype(jnp.float32)
    payload = jnp.concatenate(
        [
            new_positions[:, :, ghost_rows].reshape(per_dev * 3, ghost_count),
            heavy_f[ghost_rows][None],
        ],
        0,
    )
    beside_all = with_halo(payload[None, None], (("gx", 0), ("gy", 1)), 1)
    ghost_block = unfold(beside_all)
    pos_table = jnp.concatenate(
        [new_positions, ghost_block[: per_dev * 3].reshape(per_dev, 3, -1)], -1
    )
    heavy_table = jnp.concatenate([heavy_f, ghost_block[per_dev * 3]])
    slot_total = neighbours.shape[0]
    neighbour_pos = pos_table[:, :, neighbours]
    offsets = neighbour_pos - new_positions[:, :, None, :]
    dist_sq = jnp.sum(offsets * offsets, 1)
    distance = jnp.sqrt(dist_sq)
    in_tile = (jnp.arange(slot_total, dtype=jnp.int32)[:, None] < counts[None, :]).astype(
        jnp.float32
    )
    smooth = (
        jnp.where(distance < CUTOFF, 0.5 * (jnp.cos(math.pi * distance / CUTOFF) + 1.0), 0.0)
        * in_tile
    )
    near_heavy = heavy_table[neighbours]
    features = radial_terms(
        dist_sq, smooth * near_heavy, smooth * (1.0 - near_heavy), chi_w1.shape[2] // 2
    )
    chi = network(features, chi_w1, chi_w2, chi_w3, heavy_atoms)
    coupling = COUPLING_SCALE / slot_total * smooth / jnp.sqrt(1.0 + dist_sq)
    hardness_atom = jnp.where(heavy_atoms, hardness[0], hardness[1])
    degree = 0.5 * (jnp.sum(coupling, 1) + spread_back(coupling, neighbours, ghost_rows))
    diagonal_term = hardness_atom + degree
    right_sides = jnp.stack([-CHI_SCALE * chi, jnp.ones_like(chi)])
    solution = jnp.zeros_like(right_sides)
    residual = right_sides
    direction = right_sides
    norm_now = residual_sum(residual)
    for sweep in range(ITERS):
        outgoing = direction[:, :, ghost_rows].reshape(2 * per_dev, ghost_count)
        around_values = with_halo(outgoing[None, None], (("gx", 0), ("gy", 1)), 1)
        value_table = jnp.concatenate(
            [direction, unfold(around_values).reshape(2, per_dev, -1)], -1
        )
        forward = jnp.sum(coupling * value_table[:, :, neighbours], 2)
        backward = spread_back(coupling[None] * direction[:, :, None, :], neighbours, ghost_rows)
        applied = diagonal_term * direction - 0.5 * (forward + backward)
        curvature = lax.psum(jnp.sum(direction * applied, -1), ("gx", "gy"))[..., None]
        step_len = norm_now / curvature
        solution = solution + step_len * direction
        residual = residual - step_len * applied
        norm_next = residual_sum(residual)
        direction = residual + norm_next / norm_now * direction
        norm_now = norm_next
    totals = lax.psum(jnp.sum(solution, -1), ("gx", "gy"))
    charges = solution[0] - (totals[0] / totals[1])[:, None] * solution[1]
    energies = network(
        jnp.concatenate([features, charges[:, None, :]], 1), en_w1, en_w2, en_w3, heavy_atoms
    )
    return (new_positions, new_momenta, charges, energies)


def solution(mesh):
    placed = (
        P("bead", None, ("gx", "gy")),
        P("bead", None, ("gx", "gy")),
        P(("gx", "gy")),
        P(("gx", "gy")),
        P(None, ("gx", "gy")),
        P(("gx", "gy")),
        P(),
        P(),
        P(),
        P(),
        P(),
        P(),
        P(),
    )
    return jax.shard_map(
        on_device,
        mesh=mesh,
        in_specs=placed,
        out_specs=(
            P("bead", None, ("gx", "gy")),
            P("bead", None, ("gx", "gy")),
            P("bead", ("gx", "gy")),
            P("bead", ("gx", "gy")),
        ),
        check_vma=False,
    )
```

profile of v0, /device:TPU:0, one launch (start us, length us, event | category | flops | bytes accessed | tf_op | source)
XLA Modules:
  0.0 1984.5 jit_solution(5451067434919087645)
XLA Ops:
  5.2 14.7 all_gather.3
  37.9 7.8 pad_maximum_fusion
  45.7 121.3 %gather_fusion.2 = f32[16384,4,3]{2,1,0:T(4,128)} fusion(f32[4,3,2176]{1,0,2:T(4,128)} %pad_maximum_fusion, s32[16384]{0:T(1024)S(1)} %broadcast_clamp_fusion), kind=kCustom, calls=%fused_computation.2 | custom fusion | bytes 1638400 | tf_op jit(solution)/shard_map/gather | solution.py:174
  167.0 19.5 copy.504
  186.6 90.5 %gather_fusion.3 = f32[16384]{0:T(1024)S(1)} fusion(f32[2176]{0:T(1024)S(1)} %pad_maximum_fusion.23, s32[16384]{0:T(1024)S(1)} %broadcast_clamp_fusion), kind=kCustom, calls=%fused_computation.3 | custom fusion | bytes 196608 | tf_op jit(solution)/shard_map/gather | solution.py:185
  277.2 3.3 fusion.78
  293.4 2.1 collective-permute-start.11
  295.5 4.7 copy.505
  300.2 87.9 %scatter_custom_fusion = f32[4,2176]{0,1:T(8,128)S(1)} fusion(s32[16384]{0:T(1024)S(1)} %bitcast.282, f32[16384,4]{1,0:T(8,128)} %bitcast.257, f32[]{:T(128)} %constant.50.clone.1), kind=kCustom, calls=%fused_computation.67 | custom fusion | flops 65536 | bytes 35328 | tf_op jit(solution)/shard_map/scatter-add | solution.py:109
  391.7 4.7 copy.506
  396.4 87.9 %scatter_custom_fusion.2 = f32[8,2176]{0,1:T(8,128)S(1)} fusion(s32[16384]{0:T(1024)S(1)} %bitcast.283, f32[16384,8]{1,0:T(8,128)} %bitcast.253, f32[]{:T(128)} %constant.50.clone.1), kind=kCustom, calls=%fused_computation.65 | custom fusion | flops 131072 | bytes 70144 | tf_op jit(solution)/shard_map/scatter-add | solution.py:109
  486.0 3.2 collective-permute-start.13
  489.2 2.5 copy.434
  491.7 113.1 %gather_fusion.5 = f32[16384,2,4]{2,1,0:T(2,128)} fusion(f32[2,4,2176]{1,0,2:T(2,128)} %copy.434, s32[16384]{0:T(1024)S(1)} %broadcast_clamp_fusion), kind=kCustom, calls=%fused_computation.5 | custom fusion | bytes 1114112 | tf_op jit(solution)/shard_map/gather | solution.py:205
  604.8 13.5 copy.435
  618.9 2.9 collective-permute-start.7
  621.9 3.2 collective-permute-start.15
  629.8 38.5 %all-reduce.2 = (f32[2,4]{1,0:T(2,128)S(1)}, f32[2,4]{1,0:T(2,128)S(1)}) all-reduce(f32[2,4]{1,0:T(2,128)S(1)} %get-tuple-element.58, f32[2,4]{1,0:T(2,128)S(1)} %get-tuple-element.57), channel_id=1, replica_groups=mesh['bead'=8,'gx'=4,'gy'=4] {'gx','gy'}, use_global_device_ids=true, to_apply=%region_32.33 | all-reduce | flops 16 | bytes 128 | tf_op jit(solution)/shard_map/psum | solution.py:125
  668.5 35.4 %psum.79 = f32[2,4]{1,0:T(2,128)S(1)} all-reduce(f32[2,4]{1,0:T(2,128)S(1)} %multiply_reduce_fusion.37), channel_id=1, replica_groups=mesh['bead'=8,'gx'=4,'gy'=4] {'gx','gy'}, use_global_device_ids=true, to_apply=%region_42.43 | all-reduce | flops 8 | bytes 64 | tf_op jit(solution)/shard_map/psum | solution.py:125
  705.5 3.4 collective-permute-start.17
  713.6 4.7 copy.507
  718.3 87.9 %scatter_custom_fusion.4 = f32[8,2176]{0,1:T(8,128)S(1)} fusion(s32[16384]{0:T(1024)S(1)} %bitcast.284, f32[16384,8]{1,0:T(8,128)} %bitcast.254, f32[]{:T(128)} %constant.50.clone.1), kind=kCustom, calls=%fused_computation.63 | custom fusion | flops 131072 | bytes 70144 | tf_op jit(solution)/shard_map/scatter-add | solution.py:109
  806.5 3.5 collective-permute-start.21
  810.0 2.5 copy.446
  812.5 113.1 %gather_fusion.7 = f32[16384,2,4]{2,1,0:T(2,128)} fusion(f32[2,4,2176]{1,0,2:T(2,128)} %copy.446, s32[16384]{0:T(1024)S(1)} %broadcast_clamp_fusion), kind=kCustom, calls=%fused_computation.7 | custom fusion | bytes 1114112 | tf_op jit(solution)/shard_map/gather | solution.py:205
  925.6 13.5 copy.447
  940.0 2.4 collective-permute-start.23
  942.6 2.6 collective-permute-done.22
  947.2 40.0 %psum.80 = f32[2,4]{1,0:T(2,128)S(1)} all-reduce(f32[2,4]{1,0:T(2,128)S(1)} %multiply_reduce_fusion.36), channel_id=1, replica_groups=mesh['bead'=8,'gx'=4,'gy'=4] {'gx','gy'}, use_global_device_ids=true, to_apply=%region_47.48 | all-reduce | flops 8 | bytes 64 | tf_op jit(solution)/shard_map/psum | solution.py:208
  987.3 35.4 %psum.81 = f32[2,4]{1,0:T(2,128)S(1)} all-reduce(f32[2,4]{1,0:T(2,128)S(1)} %get-tuple-element.67), channel_id=1, replica_groups=mesh['bead'=8,'gx'=4,'gy'=4] {'gx','gy'}, use_global_device_ids=true, to_apply=%region_49.50 | all-reduce | flops 8 | bytes 64 | tf_op jit(solution)/shard_map/psum | solution.py:125
  1024.3 3.2 collective-permute-start.25
  1032.4 4.7 copy.508
  1037.1 87.9 %scatter_custom_fusion.6 = f32[8,2176]{0,1:T(8,128)S(1)} fusion(s32[16384]{0:T(1024)S(1)} %bitcast.285, f32[16384,8]{1,0:T(8,128)} %bitcast.255, f32[]{:T(128)} %constant.50.clone.1), kind=kCustom, calls=%fused_computation.61 | custom fusion | flops 131072 | bytes 70144 | tf_op jit(solution)/shard_map/scatter-add | solution.py:109
  1125.3 3.5 collective-permute-start.29
  1128.9 2.5 copy.458
  1131.4 113.1 %gather_fusion.9 = f32[16384,2,4]{2,1,0:T(2,128)} fusion(f32[2,4,2176]{1,0,2:T(2,128)} %copy.458, s32[16384]{0:T(1024)S(1)} %broadcast_clamp_fusion), kind=kCustom, calls=%fused_computation.9 | custom fusion | bytes 1114112 | tf_op jit(solution)/shard_map/gather | solution.py:205
  1244.5 13.5 copy.459
  1258.9 2.4 collective-permute-start.31
  1261.4 2.6 collective-permute-done.30
  1265.9 40.0 %psum.82 = f32[2,4]{1,0:T(2,128)S(1)} all-reduce(f32[2,4]{1,0:T(2,128)S(1)} %multiply_reduce_fusion.34), channel_id=1, replica_groups=mesh['bead'=8,'gx'=4,'gy'=4] {'gx','gy'}, use_global_device_ids=true, to_apply=%region_54.55 | all-reduce | flops 8 | bytes 64 | tf_op jit(solution)/shard_map/psum | solution.py:208
  1306.1 35.4 %psum.83 = f32[2,4]{1,0:T(2,128)S(1)} all-reduce(f32[2,4]{1,0:T(2,128)S(1)} %get-tuple-element.65), channel_id=1, replica_groups=mesh['bead'=8,'gx'=4,'gy'=4] {'gx','gy'}, use_global_device_ids=true, to_apply=%region_56.57 | all-reduce | flops 8 | bytes 64 | tf_op jit(solution)/shard_map/psum | solution.py:125
  1343.1 3.2 collective-permute-start.33
  1351.2 4.7 copy.509
  1355.8 87.9 %scatter_custom_fusion.8 = f32[8,2176]{0,1:T(8,128)S(1)} fusion(s32[16384]{0:T(1024)S(1)} %bitcast.286, f32[16384,8]{1,0:T(8,128)} %bitcast.256, f32[]{:T(128)} %constant.50.clone.1), kind=kCustom, calls=%fused_computation.59 | custom fusion | flops 131072 | bytes 70144 | tf_op jit(solution)/shard_map/scatter-add | solution.py:109
  1444.1 3.3 collective-permute-start.37
  1447.4 2.5 copy.470
  1449.9 113.1 %gather_fusion.11 = f32[16384,2,4]{2,1,0:T(2,128)} fusion(f32[2,4,2176]{1,0,2:T(2,128)} %copy.470, s32[16384]{0:T(1024)S(1)} %broadcast_clamp_fusion), kind=kCustom, calls=%fused_computation.11 | custom fusion | bytes 1114112 | tf_op jit(solution)/shard_map/gather | solution.py:205
  1563.0 13.5 copy.471
  1577.5 2.4 collective-permute-start.39
  1580.0 2.6 collective-permute-done.38
  1584.5 40.0 %psum.84 = f32[2,4]{1,0:T(2,128)S(1)} all-reduce(f32[2,4]{1,0:T(2,128)S(1)} %get-tuple-element.63), channel_id=1, replica_groups=mesh['bead'=8,'gx'=4,'gy'=4] {'gx','gy'}, use_global_device_ids=true, to_apply=%region_61.62 | all-reduce | flops 8 | bytes 64 | tf_op jit(solution)/shard_map/psum | solution.py:208
  1624.7 35.4 %psum.85 = f32[2,4]{1,0:T(2,128)S(1)} all-reduce(f32[2,4]{1,0:T(2,128)S(1)} %multiply_reduce_fusion.31), channel_id=1, replica_groups=mesh['bead'=8,'gx'=4,'gy'=4] {'gx','gy'}, use_global_device_ids=true, to_apply=%region_63.64 | all-reduce | flops 8 | bytes 64 | tf_op jit(solution)/shard_map/psum | solution.py:125
  1661.7 3.2 collective-permute-start.41
  1666.5 2.2 collective-permute-start.42
  1670.1 4.7 copy.510
  1674.7 87.9 %scatter_custom_fusion.10 = f32[8,2176]{0,1:T(8,128)S(1)} fusion(s32[16384]{0:T(1024)S(1)} %bitcast.287, f32[16384,8]{1,0:T(8,128)} %bitcast.252, f32[]{:T(128)} %constant.50.clone.1), kind=kCustom, calls=%fused_computation.57 | custom fusion | flops 131072 | bytes 70144 | tf_op jit(solution)/shard_map/scatter-add | solution.py:109
  1762.9 3.3 collective-permute-start.45
  1766.3 2.5 copy.482
  1768.8 113.1 %gather_fusion.13 = f32[16384,2,4]{2,1,0:T(2,128)} fusion(f32[2,4,2176]{1,0,2:T(2,128)} %copy.482, s32[16384]{0:T(1024)S(1)} %broadcast_clamp_fusion), kind=kCustom, calls=%fused_computation.13 | custom fusion | bytes 1114112 | tf_op jit(solution)/shard_map/gather | solution.py:205
  1881.9 13.5 copy.483
  1896.3 2.4 collective-permute-start.47
  1898.9 2.6 collective-permute-done.46
  1903.5 40.1 %psum.86 = f32[2,4]{1,0:T(2,128)S(1)} all-reduce(f32[2,4]{1,0:T(2,128)S(1)} %multiply_reduce_fusion.30), channel_id=1, replica_groups=mesh['bead'=8,'gx'=4,'gy'=4] {'gx','gy'}, use_global_device_ids=true, to_apply=%region_68.69 | all-reduce | flops 8 | bytes 64 | tf_op jit(solution)/shard_map/psum | solution.py:208
  1943.8 35.5 %psum.87 = f32[2,4]{1,0:T(2,128)S(1)} all-reduce(f32[2,4]{1,0:T(2,128)S(1)} %get-tuple-element.61), channel_id=1, replica_groups=mesh['bead'=8,'gx'=4,'gy'=4] {'gx','gy'}, use_global_device_ids=true, to_apply=%region_70.71 | all-reduce | flops 8 | bytes 64 | tf_op jit(solution)/shard_map/psum | solution.py:215
  (350 shorter events, 87.7 us)
Async XLA Ops:
  21.5 7.3 copy-start.10
  21.5 12.7 copy-start.11
  22.7 163.8 %copy-start.8 = (f32[4,3,1024]{2,0,1:T(4,128)}, f32[4,3,1024]{2,0,1:T(4,128)S(1)}, u32[]{:S(2)}) copy-start(f32[4,3,1024]{2,0,1:T(4,128)S(1)} %get-tuple-element.107) | copy-start | bytes 147460
  23.5 12.8 copy-start
  25.5 4.9 collective-permute-start
  27.1 3.7 collective-permute-start.1
  30.8 5.0 collective-permute-start.2
  32.3 4.0 collective-permute-start.3
  286.7 4.9 collective-permute-start.8
  288.3 3.6 collective-permute-start.9
  291.9 194.1 %collective-permute-start.10 = (f32[3,1,8,128]{3,2,1,0:T(8,128)S(1)}, f32[3,1,8,128]{3,2,1,0:T(8,128)S(1)}, u32[]{:S(2)}, u32[]{:S(2)}) collective-permute-start(f32[3,1,8,128]{3,2,1,0:T(8,128)S(1)} %pad_maximum_fusion.24), channel_id=1, source_target_pairs={{0,1},{1,2},{2,3},{3,0},{4,5},{5,6},{6,7},{7,4},{8,9},{9,10},{10,1... | collective-permute-start | bytes 36872 | tf_op jit(solution)/shard_map/ppermute | solution.py:27
  293.4 195.8 %collective-permute-start.11 = (f32[3,1,8,128]{3,2,1,0:T(8,128)S(1)}, f32[3,1,8,128]{3,2,1,0:T(8,128)S(1)}, u32[]{:S(2)}, u32[]{:S(2)}) collective-permute-start(f32[3,1,8,128]{3,2,1,0:T(8,128)S(1)} %pad_maximum_fusion.24), channel_id=1, source_target_pairs={{1,0},{2,1},{3,2},{0,3},{5,4},{6,5},{7,6},{4,7},{9,8},{10,9},{11,1... | collective-permute-start | bytes 36872 | tf_op jit(solution)/shard_map/ppermute | solution.py:29
  388.1 8.3 copy-start.2
  388.4 230.1 %collective-permute-start.4 = (f32[4,9,1,1,128]{4,0,3,2,1:T(4,128)S(1)}, f32[4,9,1,1,128]{4,0,3,2,1:T(4,128)S(1)}, u32[]{:S(2)}, u32[]{:S(2)}) collective-permute-start(f32[4,9,1,1,128]{4,0,3,2,1:T(4,128)S(1)} %copy.424), channel_id=1, source_target_pairs={{0,4},{4,8},{8,12},{12,0},{1,5},{5,9},{9,13},{13,1},{2,6},{6,10},{... | collective-permute-start | bytes 55304 | tf_op jit(solution)/shard_map/ppermute | solution.py:27
  389.7 228.8 %collective-permute-start.5 = (f32[4,9,1,1,128]{4,0,3,2,1:T(4,128)S(1)}, f32[4,9,1,1,128]{4,0,3,2,1:T(4,128)S(1)}, u32[]{:S(2)}, u32[]{:S(2)}) collective-permute-start(f32[4,9,1,1,128]{4,0,3,2,1:T(4,128)S(1)} %copy.424), channel_id=1, source_target_pairs={{4,0},{8,4},{12,8},{0,12},{5,1},{9,5},{13,9},{1,13},{6,2},{10,6},{... | collective-permute-start | bytes 55304 | tf_op jit(solution)/shard_map/ppermute | solution.py:29
  396.4 88.0 %slice-start.1 = ((f32[4,2176]{0,1:T(8,128)}), f32[4,1024]{0,1:T(8,128)S(1)}, s32[]{:S(2)}) async-start(f32[4,2176]{0,1:T(8,128)} %copy-done.2), calls=%async_computation.1 | async-start | bytes 1048576 | tf_op jit(solution)/shard_map/slice | solution.py:120
  484.4 7.3 copy-start.6
  485.9 136.0 %collective-permute-start.12 = (f32[8,9,1,1,128]{4,0,3,2,1:T(8,128)S(1)}, f32[8,9,1,1,128]{4,0,3,2,1:T(8,128)S(1)}, u32[]{:S(2)}, u32[]{:S(2)}) collective-permute-start(f32[8,9,1,1,128]{4,0,3,2,1:T(8,128)S(1)} %copy.437), channel_id=1, source_target_pairs={{0,4},{4,8},{8,12},{12,0},{1,5},{5,9},{9,13},{13,1},{2,6},{6,10},{... | collective-permute-start | bytes 110600 | tf_op jit(solution)/shard_map/ppermute | solution.py:27
  486.0 135.9 %collective-permute-start.13 = (f32[8,9,1,1,128]{4,0,3,2,1:T(8,128)S(1)}, f32[8,9,1,1,128]{4,0,3,2,1:T(8,128)S(1)}, u32[]{:S(2)}, u32[]{:S(2)}) collective-permute-start(f32[8,9,1,1,128]{4,0,3,2,1:T(8,128)S(1)} %copy.437), channel_id=1, source_target_pairs={{4,0},{8,4},{12,8},{0,12},{5,1},{9,5},{13,9},{1,13},{6,2},{10,6},{... | collective-permute-start | bytes 110600 | tf_op jit(solution)/shard_map/ppermute | solution.py:29
  604.8 20.5 %copy-start.7 = (f32[4,1024]{0,1:T(8,128)S(1)}, f32[4,1024]{0,1:T(8,128)}, u32[]{:S(2)}) copy-start(f32[4,1024]{0,1:T(8,128)} %copy.428) | copy-start | bytes 49156
  604.8 23.2 %slice-start.5 = ((f32[8,2176]{0,1:T(8,128)}), f32[8,1024]{0,1:T(8,128)S(1)}, s32[]{:S(2)}) async-start(f32[8,2176]{0,1:T(8,128)} %copy-done.6), calls=%async_computation.5 | async-start | bytes 1048576 | tf_op jit(solution)/shard_map/slice | solution.py:120
  618.5 6.6 collective-permute-start.6
  618.9 6.3 collective-permute-start.7
  621.8 6.1 collective-permute-start.14
  621.9 6.0 collective-permute-start.15
  705.5 4.8 collective-permute-start.16
  705.5 4.8 collective-permute-start.17
  710.3 99.6 %collective-permute-start.18 = (f32[3,1,8,128]{3,2,1,0:T(8,128)S(1)}, f32[3,1,8,128]{3,2,1,0:T(8,128)S(1)}, u32[]{:S(2)}, u32[]{:S(2)}) collective-permute-start(f32[3,1,8,128]{3,2,1,0:T(8,128)S(1)} %pad_maximum_fusion.25), channel_id=1, source_target_pairs={{0,1},{1,2},{2,3},{3,0},{4,5},{5,6},{6,7},{7,4},{8,9},{9,10},{10,1... | collective-permute-start | bytes 36872 | tf_op jit(solution)/shard_map/ppermute | solution.py:27
  712.3 97.6 %collective-permute-start.19 = (f32[3,1,8,128]{3,2,1,0:T(8,128)S(1)}, f32[3,1,8,128]{3,2,1,0:T(8,128)S(1)}, u32[]{:S(2)}, u32[]{:S(2)}) collective-permute-start(f32[3,1,8,128]{3,2,1,0:T(8,128)S(1)} %pad_maximum_fusion.25), channel_id=1, source_target_pairs={{1,0},{2,1},{3,2},{0,3},{5,4},{6,5},{7,6},{4,7},{9,8},{10,9},{11,1... | collective-permute-start | bytes 36872 | tf_op jit(solution)/shard_map/ppermute | solution.py:29
  806.4 132.7 %collective-permute-start.20 = (f32[8,9,1,1,128]{4,0,3,2,1:T(8,128)S(1)}, f32[8,9,1,1,128]{4,0,3,2,1:T(8,128)S(1)}, u32[]{:S(2)}, u32[]{:S(2)}) collective-permute-start(f32[8,9,1,1,128]{4,0,3,2,1:T(8,128)S(1)} %copy.449), channel_id=1, source_target_pairs={{0,4},{4,8},{8,12},{12,0},{1,5},{5,9},{9,13},{13,1},{2,6},{6,10},{... | collective-permute-start | bytes 110600 | tf_op jit(solution)/shard_map/ppermute | solution.py:27
  806.5 132.6 %collective-permute-start.21 = (f32[8,9,1,1,128]{4,0,3,2,1:T(8,128)S(1)}, f32[8,9,1,1,128]{4,0,3,2,1:T(8,128)S(1)}, u32[]{:S(2)}, u32[]{:S(2)}) collective-permute-start(f32[8,9,1,1,128]{4,0,3,2,1:T(8,128)S(1)} %copy.449), channel_id=1, source_target_pairs={{4,0},{8,4},{12,8},{0,12},{5,1},{9,5},{13,9},{1,13},{6,2},{10,6},{... | collective-permute-start | bytes 110600 | tf_op jit(solution)/shard_map/ppermute | solution.py:29
  925.6 19.7 slice-start.2
  939.1 6.1 collective-permute-start.22
  940.0 5.2 collective-permute-start.23
  1024.3 4.8 collective-permute-start.24
  1024.3 4.8 collective-permute-start.25
  1029.1 99.7 %collective-permute-start.26 = (f32[3,1,8,128]{3,2,1,0:T(8,128)S(1)}, f32[3,1,8,128]{3,2,1,0:T(8,128)S(1)}, u32[]{:S(2)}, u32[]{:S(2)}) collective-permute-start(f32[3,1,8,128]{3,2,1,0:T(8,128)S(1)} %pad_maximum_fusion.26), channel_id=1, source_target_pairs={{0,1},{1,2},{2,3},{3,0},{4,5},{5,6},{6,7},{7,4},{8,9},{9,10},{10,1... | collective-permute-start | bytes 36872 | tf_op jit(solution)/shard_map/ppermute | solution.py:27
  1031.2 97.6 %collective-permute-start.27 = (f32[3,1,8,128]{3,2,1,0:T(8,128)S(1)}, f32[3,1,8,128]{3,2,1,0:T(8,128)S(1)}, u32[]{:S(2)}, u32[]{:S(2)}) collective-permute-start(f32[3,1,8,128]{3,2,1,0:T(8,128)S(1)} %pad_maximum_fusion.26), channel_id=1, source_target_pairs={{1,0},{2,1},{3,2},{0,3},{5,4},{6,5},{7,6},{4,7},{9,8},{10,9},{11,1... | collective-permute-start | bytes 36872 | tf_op jit(solution)/shard_map/ppermute | solution.py:29
  1125.2 132.7 %collective-permute-start.28 = (f32[8,9,1,1,128]{4,0,3,2,1:T(8,128)S(1)}, f32[8,9,1,1,128]{4,0,3,2,1:T(8,128)S(1)}, u32[]{:S(2)}, u32[]{:S(2)}) collective-permute-start(f32[8,9,1,1,128]{4,0,3,2,1:T(8,128)S(1)} %copy.461), channel_id=1, source_target_pairs={{0,4},{4,8},{8,12},{12,0},{1,5},{5,9},{9,13},{13,1},{2,6},{6,10},{... | collective-permute-start | bytes 110600 | tf_op jit(solution)/shard_map/ppermute | solution.py:27
  1125.3 132.7 %collective-permute-start.29 = (f32[8,9,1,1,128]{4,0,3,2,1:T(8,128)S(1)}, f32[8,9,1,1,128]{4,0,3,2,1:T(8,128)S(1)}, u32[]{:S(2)}, u32[]{:S(2)}) collective-permute-start(f32[8,9,1,1,128]{4,0,3,2,1:T(8,128)S(1)} %copy.461), channel_id=1, source_target_pairs={{4,0},{8,4},{12,8},{0,12},{5,1},{9,5},{13,9},{1,13},{6,2},{10,6},{... | collective-permute-start | bytes 110600 | tf_op jit(solution)/shard_map/ppermute | solution.py:29
  1244.5 19.7 slice-start.3
  1258.0 6.0 collective-permute-start.30
  1258.9 5.1 collective-permute-start.31
  1343.0 4.8 collective-permute-start.32
  1343.1 4.8 collective-permute-start.33
  1347.9 99.5 %collective-permute-start.34 = (f32[3,1,8,128]{3,2,1,0:T(8,128)S(1)}, f32[3,1,8,128]{3,2,1,0:T(8,128)S(1)}, u32[]{:S(2)}, u32[]{:S(2)}) collective-permute-start(f32[3,1,8,128]{3,2,1,0:T(8,128)S(1)} %pad_maximum_fusion.27), channel_id=1, source_target_pairs={{0,1},{1,2},{2,3},{3,0},{4,5},{5,6},{6,7},{7,4},{8,9},{9,10},{10,1... | collective-permute-start | bytes 36872 | tf_op jit(solution)/shard_map/ppermute | solution.py:27
  1349.9 97.5 %collective-permute-start.35 = (f32[3,1,8,128]{3,2,1,0:T(8,128)S(1)}, f32[3,1,8,128]{3,2,1,0:T(8,128)S(1)}, u32[]{:S(2)}, u32[]{:S(2)}) collective-permute-start(f32[3,1,8,128]{3,2,1,0:T(8,128)S(1)} %pad_maximum_fusion.27), channel_id=1, source_target_pairs={{1,0},{2,1},{3,2},{0,3},{5,4},{6,5},{7,6},{4,7},{9,8},{10,9},{11,1... | collective-permute-start | bytes 36872 | tf_op jit(solution)/shard_map/ppermute | solution.py:29
  1444.0 132.5 %collective-permute-start.36 = (f32[8,9,1,1,128]{4,0,3,2,1:T(8,128)S(1)}, f32[8,9,1,1,128]{4,0,3,2,1:T(8,128)S(1)}, u32[]{:S(2)}, u32[]{:S(2)}) collective-permute-start(f32[8,9,1,1,128]{4,0,3,2,1:T(8,128)S(1)} %copy.473), channel_id=1, source_target_pairs={{0,4},{4,8},{8,12},{12,0},{1,5},{5,9},{9,13},{13,1},{2,6},{6,10},{... | collective-permute-start | bytes 110600 | tf_op jit(solution)/shard_map/ppermute | solution.py:27
  1444.1 132.5 %collective-permute-start.37 = (f32[8,9,1,1,128]{4,0,3,2,1:T(8,128)S(1)}, f32[8,9,1,1,128]{4,0,3,2,1:T(8,128)S(1)}, u32[]{:S(2)}, u32[]{:S(2)}) collective-permute-start(f32[8,9,1,1,128]{4,0,3,2,1:T(8,128)S(1)} %copy.473), channel_id=1, source_target_pairs={{4,0},{8,4},{12,8},{0,12},{5,1},{9,5},{13,9},{1,13},{6,2},{10,6},{... | collective-permute-start | bytes 110600 | tf_op jit(solution)/shard_map/ppermute | solution.py:29
  1563.0 19.7 slice-start.4
  1576.5 88.4 %copy-start.12 = (f32[2,25,31]{2,0,1:T(2,128)S(1)}, f32[2,25,31]{2,0,1:T(2,128)}, u32[]{:S(2)}) copy-start(f32[2,25,31]{2,0,1:T(2,128)} %param.23) | copy-start | bytes 18604
  1576.5 93.5 %copy-start.13 = (f32[2,25,25]{2,0,1:T(2,128)S(1)}, f32[2,25,25]{2,0,1:T(2,128)}, u32[]{:S(2)}) copy-start(f32[2,25,25]{2,0,1:T(2,128)} %param.24) | copy-start | bytes 15004
  1576.6 6.0 collective-permute-start.38
  1577.5 5.1 collective-permute-start.39
  1661.7 4.8 collective-permute-start.40
  1661.7 4.8 collective-permute-start.41
  1666.5 99.7 %collective-permute-start.42 = (f32[3,1,8,128]{3,2,1,0:T(8,128)S(1)}, f32[3,1,8,128]{3,2,1,0:T(8,128)S(1)}, u32[]{:S(2)}, u32[]{:S(2)}) collective-permute-start(f32[3,1,8,128]{3,2,1,0:T(8,128)S(1)} %pad_maximum_fusion.28), channel_id=1, source_target_pairs={{0,1},{1,2},{2,3},{3,0},{4,5},{5,6},{6,7},{7,4},{8,9},{9,10},{10,1... | collective-permute-start | bytes 36872 | tf_op jit(solution)/shard_map/ppermute | solution.py:27
  1668.7 97.5 %collective-permute-start.43 = (f32[3,1,8,128]{3,2,1,0:T(8,128)S(1)}, f32[3,1,8,128]{3,2,1,0:T(8,128)S(1)}, u32[]{:S(2)}, u32[]{:S(2)}) collective-permute-start(f32[3,1,8,128]{3,2,1,0:T(8,128)S(1)} %pad_maximum_fusion.28), channel_id=1, source_target_pairs={{1,0},{2,1},{3,2},{0,3},{5,4},{6,5},{7,6},{4,7},{9,8},{10,9},{11,1... | collective-permute-start | bytes 36872 | tf_op jit(solution)/shard_map/ppermute | solution.py:29
  1762.9 132.5 %collective-permute-start.44 = (f32[8,9,1,1,128]{4,0,3,2,1:T(8,128)S(1)}, f32[8,9,1,1,128]{4,0,3,2,1:T(8,128)S(1)}, u32[]{:S(2)}, u32[]{:S(2)}) collective-permute-start(f32[8,9,1,1,128]{4,0,3,2,1:T(8,128)S(1)} %copy.485), channel_id=1, source_target_pairs={{0,4},{4,8},{8,12},{12,0},{1,5},{5,9},{9,13},{13,1},{2,6},{6,10},{... | collective-permute-start | bytes 110600 | tf_op jit(solution)/shard_map/ppermute | solution.py:27
  1762.9 132.5 %collective-permute-start.45 = (f32[8,9,1,1,128]{4,0,3,2,1:T(8,128)S(1)}, f32[8,9,1,1,128]{4,0,3,2,1:T(8,128)S(1)}, u32[]{:S(2)}, u32[]{:S(2)}) collective-permute-start(f32[8,9,1,1,128]{4,0,3,2,1:T(8,128)S(1)} %copy.485), channel_id=1, source_target_pairs={{4,0},{8,4},{12,8},{0,12},{5,1},{9,5},{13,9},{1,13},{6,2},{10,6},{... | collective-permute-start | bytes 110600 | tf_op jit(solution)/shard_map/ppermute | solution.py:29
  1881.9 19.7 slice-start
  1895.4 6.0 collective-permute-start.46
  1896.3 5.1 collective-permute-start.47
  1903.2 78.6 %copy-start.15 = (f32[2,25]{1,0:T(2,128)S(1)}, f32[2,25]{1,0:T(2,128)}, u32[]{:S(2)}) copy-start(f32[2,25]{1,0:T(2,128)} %param.25) | copy-start | bytes 604
  (8 other events, 45.1 us)
where the time goes:
time: 1990 us; the launch traced here: 1980 us
  local copies, waits for them, and re-layouts  924 us (46%)
  other arithmetic  556 us (28%)
  blocking collectives  391 us (20%)
  starting transfers between devices  80.2 us (4%)
  waiting for transfers between devices  23.5 us (1%)
    gather x10, local copies, waits for them, and re-layouts, on_device(): forward = jnp.sum(coupling * value_table[:, :, neighbours], 2)  633 us
    scatter-add x6, other arithmetic, spread_back(): jnp.zeros((layers, atoms + 9 * ghost_count), jnp.float32).at[:, neighbours]  527 us
    psum x5, blocking collectives, residual_sum(): return lax.psum(jnp.sum(residual * residual, -1), ('gx', 'gy'))[..., None]  180 us
    psum x4, blocking collectives, on_device(): lax.psum(jnp.sum(direction * applied, -1), ('gx', 'gy'))[..., None]  160 us
    gather x2, local copies, waits for them, and re-layouts, on_device(): neighbour_pos = pos_table[:, :, neighbours]  141 us
    gather x2, local copies, waits for them, and re-layouts, on_device(): near_heavy = heavy_table[neighbours]  90.6 us
    ppermute x24, starting transfers between devices, with_halo(): lax.ppermute(head, axis, [((i + 1) % count, i) for i in range(count)])  59.8 us
  transfers between devices with their start and end apart: 48, of which 15 were waited for; matrix products, arithmetic and copies ran while one was open for 61% of the time, Pallas kernels for 0%

commit v1 on v0

v1 whole, which is shorter than its diff:
```python
import functools
import math

import jax
import jax.numpy as jnp
import numpy as np
from jax import lax
from jax.experimental import pallas as pl
from jax.experimental.pallas import tpu as pltpu
from jax.sharding import PartitionSpec as P

MESH = pl.DeviceIdType.MESH
F32 = jnp.float32
BF16 = jnp.bfloat16
HIGHEST = lax.Precision.HIGHEST
ITERS = 5
STEP = 0.5
TOP_FREQ = 80.0
CUTOFF = 4.0
HEAVY_MASS = 16.0
CHI_SCALE = 4.0
LANES = 128
BEADS = 32
GROUPS = 8
PER = 4
ATOMS = 1024
CHUNKS = ATOMS // LANES
SLOTS = 16
TABLE = ATOMS + 9 * LANES
HALF = 15
FEATS = 2 * HALF
SIDE = 4
BRICKS = SIDE * SIDE
BAND = 16
WIDE = 256
BLOCKS = -(-TABLE // WIDE)
VMEM_LIMIT = 60 * 1024 * 1024


def propagator():
    k = np.arange(BEADS)
    omega = TOP_FREQ * np.sin(math.pi * k / BEADS)
    cosine = np.cos(omega * STEP)
    sine = np.sin(omega * STEP)
    drift = np.where(k > 0, TOP_FREQ * sine / np.where(k > 0, omega, 1.0), TOP_FREQ * STEP)
    restoring = -(omega / TOP_FREQ) * sine
    gap = (k[:, None] - k[None, :]) % BEADS

    def spread(weights):
        line = (weights[None, :] * np.cos(2 * math.pi * k[:, None] * k[None, :] / BEADS)).sum(1) / BEADS
        return line[gap]

    keep, push, pull = spread(cosine), spread(drift), spread(restoring)
    zero = np.zeros_like(keep)
    plain = np.block([[keep, zero], [zero, keep]])
    massive = np.block([[zero, push], [pull, zero]])
    order = np.array([half * BEADS + g * PER + b for g in range(GROUPS) for half in range(2) for b in range(PER)])
    both = np.concatenate([plain[order][:, order], massive[order][:, order]], 0)
    return both.astype(np.float32)


def sublanes(shape):
    return lax.broadcasted_iota(jnp.int32, shape, 0)


def lane_take(table, lane):
    return jnp.take_along_axis(table, lane, axis=1, mode="promise_in_bounds")


def row_bits(rows, count):
    return [(rows & (LANES << bit)) != 0 for bit in range(count)]


def pick(parts, bits):
    level = 0
    while len(parts) > 1:
        nxt = [
            jnp.where(bits[level], parts[i + 1], parts[i]) for i in range(0, len(parts) - 1, 2)
        ]
        if len(parts) % 2:
            nxt.append(parts[-1])
        parts = nxt
        level += 1
    return parts[0]


def brick_at(dx, dy):
    return {
        "gx": lax.rem(lax.axis_index("gx") + dx + SIDE, SIDE),
        "gy": lax.rem(lax.axis_index("gy") + dy + SIDE, SIDE),
    }


AROUND = [(a, c) for a in range(3) for c in range(3) if (a, c) != (1, 1)]


def propagate_kernel(
    matrix_ref,
    pos_ref,
    mom_ref,
    types_ref,
    ghost_ref,
    newpos_ref,
    newmom_ref,
    tab_ref,
    stage,
    modes,
    moved,
    back,
    lent,
    send1,
    recv1,
    send2,
    recv2,
    send3,
    recv3,
):
    me = lax.axis_index("bead")
    width = 3 * LANES
    barrier = pltpu.get_barrier_semaphore()
    for o in range(1, GROUPS):
        pl.semaphore_signal(
            barrier, inc=1, device_id={"bead": lax.rem(me + o, GROUPS)}, device_id_type=MESH
        )
    for a, c in AROUND:
        pl.semaphore_signal(barrier, inc=1, device_id=brick_at(a - 1, c - 1), device_id_type=MESH)
    sub = sublanes((8, LANES))
    low = sub < PER
    for d in range(CHUNKS):
        for c in range(3):
            at = d * width + c * LANES
            stage[0:PER, at : at + LANES] = pos_ref[:, c, d * LANES : (d + 1) * LANES]
            stage[PER:8, at : at + LANES] = mom_ref[:, c, d * LANES : (d + 1) * LANES]
    pl.semaphore_wait(barrier, GROUPS - 1 + len(AROUND))
    copies = []
    for o in range(1, GROUPS):
        to = lax.rem(me + o, GROUPS)
        cp = pltpu.make_async_remote_copy(
            src_ref=stage.at[:, pl.ds(pl.multiple_of(to * width, LANES), width)],
            dst_ref=modes.at[pl.ds(pl.multiple_of(me * 8, 8), 8), :],
            send_sem=send1.at[o],
            recv_sem=recv1.at[o],
            device_id={"bead": to},
            device_id_type=MESH,
        )
        cp.start()
        copies.append(cp)
    mine = pl.ds(pl.multiple_of(me * 8, 8), 8)
    my_lanes = pl.ds(pl.multiple_of(me * width, LANES), width)
    modes[mine, :] = stage[:, my_lanes]
    heavy = jnp.where(types_ref[...] == 0, 1.0, 0.0)
    ghost_rows = jnp.broadcast_to(ghost_ref[...], (8, LANES))
    ghost_lane = ghost_rows & (LANES - 1)
    ghost_bits = row_bits(ghost_rows, 3)
    for d in range(CHUNKS):
        tab_ref[3, :, d * LANES : (d + 1) * LANES] = jnp.broadcast_to(
            heavy[:, d * LANES : (d + 1) * LANES], (8, LANES)
        )
    my_types = types_ref[:, pl.ds(pl.multiple_of(me * LANES, LANES), LANES)]
    mass = jnp.where(my_types == 0, HEAVY_MASS, 1.0)
    mass = jnp.broadcast_to(mass, (8, LANES))
    factor = jnp.where(low, 1.0 / mass, mass)
    factor = jnp.concatenate([factor] * 3, 1)
    for cp in copies:
        cp.wait()
    both = jnp.dot(matrix_ref[...], modes[...], precision=HIGHEST, preferred_element_type=F32)
    for g in range(GROUPS):
        rows = slice(g * 8, g * 8 + 8)
        moved[rows, :] = both[rows] + both[64 + g * 8 : 72 + g * 8] * factor
    copies = []
    for o in range(1, GROUPS):
        to = lax.rem(me + o, GROUPS)
        cp = pltpu.make_async_remote_copy(
            src_ref=moved.at[pl.ds(pl.multiple_of(to * 8, 8), 8), :],
            dst_ref=back.at[:, my_lanes],
            send_sem=send2.at[o],
            recv_sem=recv2.at[o],
            device_id={"bead": to},
            device_id_type=MESH,
        )
        cp.start()
        copies.append(cp)
    back[:, my_lanes] = moved[mine, :]
    for cp in copies:
        cp.wait()
    for c in range(3):
        for d in range(CHUNKS):
            at = d * width + c * LANES
            v = back[:, at : at + LANES]
            newpos_ref[:, c, d * LANES : (d + 1) * LANES] = v[0:PER]
            newmom_ref[:, c, d * LANES : (d + 1) * LANES] = v[PER:8]
            tab_ref[c, :, d * LANES : (d + 1) * LANES] = jnp.where(low, v, pltpu.roll(v, PER, 0))
    for c in range(4):
        lent[c] = pick(
            [lane_take(tab_ref[c, :, d * LANES : (d + 1) * LANES], ghost_lane) for d in range(CHUNKS)],
            ghost_bits,
        )
    copies = []
    for n, (a, c) in enumerate(AROUND):
        at = ATOMS + (3 * a + c) * LANES
        cp = pltpu.make_async_remote_copy(
            src_ref=lent,
            dst_ref=tab_ref.at[:, :, at : at + LANES],
            send_sem=send3.at[n],
            recv_sem=recv3.at[n],
            device_id=brick_at(1 - a, 1 - c),
            device_id_type=MESH,
        )
        cp.start()
        copies.append(cp)
    at = ATOMS + 4 * LANES
    tab_ref[:, :, at : at + LANES] = lent[...]
    for cp in copies:
        cp.wait()


def network(features, w1_ref, w2_ref, w3_ref, heavy):
    results = []
    for e in range(2):
        h = jnp.tanh(jnp.dot(w1_ref[e], features, precision=HIGHEST, preferred_element_type=F32))
        h = jnp.tanh(jnp.dot(w2_ref[e], h, precision=HIGHEST, preferred_element_type=F32))
        results.append(
            jnp.dot(w3_ref[e : e + 1, :], h, precision=HIGHEST, preferred_element_type=F32)
        )
    return jnp.where(heavy, results[0], results[1])


def features_kernel(
    tab_ref,
    idx_ref,
    counts_ref,
    types_ref,
    w1_ref,
    w2_ref,
    w3_ref,
    coup_ref,
    feat_ref,
    rhs_ref,
    pairs,
):
    sub = sublanes((8, LANES))
    low = sub < PER
    low_all = sublanes((8, ATOMS)) < PER
    for kp in range(SLOTS // 2):
        pairs[kp] = jnp.where(
            low_all,
            jnp.broadcast_to(idx_ref[2 * kp : 2 * kp + 1, :], (8, ATOMS)),
            jnp.broadcast_to(idx_ref[2 * kp + 1 : 2 * kp + 2, :], (8, ATOMS)),
        )
    slot_off = jnp.where(low, 0, 1)
    cos_scale = (math.pi / (2.0 * CUTOFF)) ** 2
    cos_terms = [(-1.0) ** n * cos_scale**n / math.factorial(2 * n) for n in range(8)]
    feat_ref[...] = jnp.zeros_like(feat_ref)

    def chunk_step(ci, carry):
        lanes = pl.ds(pl.multiple_of(ci * LANES, LANES), LANES)
        own = [tab_ref[c, :, lanes] for c in range(3)]
        count = jnp.broadcast_to(counts_ref[:, lanes], (8, LANES))

        def pair_step(kp, sums):
            rows = pairs[kp, :, lanes]
            lane = rows & (LANES - 1)
            bits = row_bits(rows, 5)
            near = [
                pick(
                    [
                        lane_take(tab_ref[c, :, t * LANES : (t + 1) * LANES], lane)
                        for t in range(TABLE // LANES)
                    ],
                    bits,
                )
                for c in range(4)
            ]
            dist_sq = sum((near[c] - own[c]) ** 2 for c in range(3))
            close = jnp.minimum(dist_sq, CUTOFF * CUTOFF)
            wave = jnp.full_like(close, cos_terms[-1])
            for term in cos_terms[-2::-1]:
                wave = wave * close + term
            used = ((2 * kp + slot_off) < count) & (dist_sq < CUTOFF * CUTOFF)
            smooth = jnp.where(used, wave * wave, 0.0)
            heavy_w = smooth * near[3]
            light_w = smooth - heavy_w
            coupling = smooth * lax.rsqrt(1.0 + dist_sq)
            turned = pltpu.roll(coupling, PER, 0)
            coup_ref[2 * kp, :, lanes] = jnp.where(low, coupling, turned)
            coup_ref[2 * kp + 1, :, lanes] = jnp.where(low, turned, coupling)
            out = []
            for s in range(HALF):
                eta = 0.2 * 20.0 ** (s / (HALF - 1))
                falloff = jnp.exp(dist_sq * (-eta))
                out.append(sums[2 * s] + heavy_w * falloff)
                out.append(sums[2 * s + 1] + light_w * falloff)
            return tuple(out)

        sums = lax.fori_loop(
            0, SLOTS // 2, pair_step, tuple(jnp.zeros((8, LANES), F32) for _ in range(FEATS))
        )
        for s in range(HALF):
            for e in range(2):
                v = sums[2 * s + e]
                v = jnp.log(1.0 + (v + pltpu.roll(v, PER, 0)))
                row = (e * HALF + s) * PER
                feat_ref[ci, row : row + PER, :] = v[0:PER]
        return carry

    lax.fori_loop(0, CHUNKS, chunk_step, 0)
    heavy = types_ref[...] == 0
    for b in range(PER):
        f = jnp.concatenate(
            [feat_ref[d, pl.ds(b, FEATS, stride=PER), :] for d in range(CHUNKS)], 1
        )
        chi = network(f, w1_ref, w2_ref, w3_ref, heavy)
        rhs_ref[b : b + 1, :] = -CHI_SCALE * chi
    rhs_ref[PER:8, :] = jnp.ones((PER, ATOMS), F32)


def solve_kernel(
    hardness_ref,
    rhs_ref,
    coup_ref,
    idx_ref,
    types_ref,
    ghost_ref,
    charge_ref,
    rows_all,
    onehot,
    ghost_onehot,
    residual,
    direction,
    image,
    total,
    degree,
    table,
    scattered,
    spread,
    lent,
    backin,
    parts,
    send1,
    recv1,
    send2,
    recv2,
    send3,
    recv3,
):
    gx, gy = lax.axis_index("gx"), lax.axis_index("gy")
    me = gx * SIDE + gy
    others = [(o // SIDE, o % SIDE) for o in range(1, BRICKS)]
    barrier = pltpu.get_barrier_semaphore()
    for dx, dy in others:
        pl.semaphore_signal(barrier, inc=1, device_id=brick_at(dx, dy), device_id_type=MESH)
    sub = sublanes((8, LANES))
    low = sub < PER
    ghost_rows = jnp.broadcast_to(ghost_ref[...], (8, LANES))
    ghost_lane = ghost_rows & (LANES - 1)
    ghost_bits = row_bits(ghost_rows, 3)
    within = sublanes((WIDE, ATOMS)).astype(F32).astype(BF16)

    for k in range(SLOTS):
        rows_all[k] = jnp.broadcast_to(idx_ref[k : k + 1, :], (8, ATOMS))

    def build(k, carry):
        wide = (rows_all[k] & (WIDE - 1)).astype(F32)
        wide = jnp.concatenate([wide, wide], 0).astype(BF16)
        wide = jnp.concatenate([wide] * (WIDE // BAND), 0)
        onehot[k] = jnp.where(within == wide, 1.0, 0.0).astype(BF16)
        return carry

    lax.fori_loop(0, SLOTS, build, 0)
    for d in range(CHUNKS):
        rows = sublanes((LANES, LANES)) + d * LANES
        hit = rows == jnp.broadcast_to(ghost_ref[...], (LANES, LANES))
        ghost_onehot[d * LANES : (d + 1) * LANES, :] = jnp.where(hit, 1.0, 0.0).astype(BF16)
    hard = jnp.where(types_ref[...] == 0, hardness_ref[0], hardness_ref[1])
    residual[...] = rhs_ref[...]
    direction[...] = jnp.zeros_like(direction)
    image[...] = jnp.zeros_like(image)
    total[...] = jnp.zeros_like(total)
    degree[...] = jnp.zeros_like(degree)
    pl.semaphore_wait(barrier, len(others))

    def split(v):
        top = v.astype(BF16).astype(F32)
        return jnp.concatenate([top, v - top], 0).astype(BF16)

    def sweep(it, state):
        norm_prev, curve_prev, sum_prev, sum_total = state
        parity = lax.rem(it, 2)
        lent[0] = pick(
            [lane_take(residual[:, d * LANES : (d + 1) * LANES], ghost_lane) for d in range(CHUNKS)],
            ghost_bits,
        )
        first = []
        for n, (a, c) in enumerate(AROUND):
            at = ATOMS + (3 * a + c) * LANES
            cp = pltpu.make_async_remote_copy(
                src_ref=lent.at[0],
                dst_ref=table.at[:, at : at + LANES],
                send_sem=send1.at[n],
                recv_sem=recv1.at[n],
                device_id=brick_at(1 - a, 1 - c),
                device_id_type=MESH,
            )
            cp.start()
            first.append(cp)
        table[:, 0:ATOMS] = residual[...]
        table[:, ATOMS + 4 * LANES : ATOMS + 5 * LANES] = lent[0]
        scattered[...] = jnp.zeros_like(scattered)

        def scatter(k, carry):
            terms = split(coup_ref[k] * residual[...])
            block = (rows_all[k] >> 8).astype(F32)
            block = jnp.concatenate([block, block], 0).astype(BF16)
            zero = jnp.zeros_like(terms)
            tall = jnp.concatenate([jnp.where(block == b, terms, zero) for b in range(BLOCKS)], 0)
            scattered[...] += lax.dot_general(
                tall, onehot[k], (((1,), (1,)), ((), ())), preferred_element_type=F32
            )
            return carry

        lax.fori_loop(0, SLOTS, scatter, 0)
        for t in range(9):
            n = CHUNKS + t
            row, col = (n // 2) * BAND, (n % 2) * LANES
            spread[t] = (
                scattered[row : row + 8, col : col + LANES]
                + scattered[row + 8 : row + 16, col : col + LANES]
            )
        second = []
        for n, (a, c) in enumerate(AROUND):
            t = 3 * a + c
            cp = pltpu.make_async_remote_copy(
                src_ref=spread.at[t],
                dst_ref=backin.at[t],
                send_sem=send2.at[n],
                recv_sem=recv2.at[n],
                device_id=brick_at(a - 1, c - 1),
                device_id_type=MESH,
            )
            cp.start()
            second.append(cp)
        for cp in first:
            cp.wait()

        def gather(k, acc):
            out = []
            for d in range(CHUNKS):
                lanes = slice(d * LANES, (d + 1) * LANES)
                rows = rows_all[k, :, lanes]
                lane = rows & (LANES - 1)
                near = pick(
                    [
                        lane_take(table[:, t * LANES : (t + 1) * LANES], lane)
                        for t in range(TABLE // LANES)
                    ],
                    row_bits(rows, 5),
                )
                out.append(acc[d] + coup_ref[k, :, lanes] * near)
            return tuple(out)

        forward = lax.fori_loop(
            0, SLOTS, gather, tuple(jnp.zeros((8, LANES), F32) for _ in range(CHUNKS))
        )
        forward = jnp.concatenate(forward, 1)
        for cp in second:
            cp.wait()
        received = spread[4]
        for a, c in AROUND:
            received = received + backin[3 * a + c]
        returned = lax.dot_general(
            split(received), ghost_onehot[...], (((1,), (1,)), ((), ())), preferred_element_type=F32
        )
        pieces = []
        for d in range(CHUNKS):
            row, col = (d // 2) * BAND, (d % 2) * LANES
            pieces.append(
                scattered[row : row + 8, col : col + LANES]
                + scattered[row + 8 : row + 16, col : col + LANES]
            )
        around = forward + jnp.concatenate(pieces, 1) + returned[0:8] + returned[8:16]
        low_all = sublanes((8, ATOMS)) < PER
        fresh = 0.5 * jnp.where(low_all, pltpu.roll(around, PER, 0), around)
        deg = jnp.where(it == 0, fresh, degree[...])
        degree[...] = deg
        r = residual[...]
        w = (hard + deg) * r - 0.5 * around

        def lanes_sum(v):
            return jnp.sum(v, axis=1, keepdims=True)

        s_prev = image[...]
        lane_id = lax.broadcasted_iota(jnp.int32, (8, LANES), 1)
        dots = [lanes_sum(r * r), lanes_sum(r * w), lanes_sum(r * s_prev), lanes_sum(r)]
        mine = jnp.where(
            lane_id == 0, dots[0], jnp.where(lane_id == 1, dots[1], jnp.where(lane_id == 2, dots[2], dots[3]))
        )
        parts[parity, me] = mine
        third = []
        for n, (dx, dy) in enumerate(others):
            cp = pltpu.make_async_remote_copy(
                src_ref=parts.at[parity, me],
                dst_ref=parts.at[parity, me],
                send_sem=send3.at[parity, n],
                recv_sem=recv3.at[parity, n],
                device_id=brick_at(dx, dy),
                device_id_type=MESH,
            )
            cp.start()
            third.append(cp)
        for cp in third:
            cp.wait()
        whole = parts[parity, 0]
        for n in range(1, BRICKS):
            whole = whole + parts[parity, n]
        norm, rw, rs, r_sum = (whole[:, n : n + 1] for n in range(4))
        beta = jnp.where(it == 0, 0.0, norm / norm_prev)
        curve = rw + 2.0 * beta * rs + beta * beta * curve_prev
        alpha = norm / curve
        p = r + beta * direction[...]
        s = w + beta * s_prev
        direction[...] = p
        image[...] = s
        total[...] += alpha * p
        residual[...] = r - alpha * s
        p_sum = r_sum + beta * sum_prev
        return norm, curve, p_sum, sum_total + alpha * p_sum

    zero = jnp.zeros((8, 1), F32)
    state = lax.fori_loop(0, ITERS, sweep, (zero + 1.0, zero, zero, zero))
    sums = state[3]
    ratio = sums[0:PER] / sums[PER:8]
    charge_ref[...] = total[0:PER, :] - ratio * total[PER:8, :]


def energies_kernel(feat_ref, charge_ref, types_ref, w1_ref, w2_ref, w3_ref, out_ref, full):
    full[...] = feat_ref[...]
    for d in range(CHUNKS):
        full[d, FEATS * PER : (FEATS + 1) * PER, :] = charge_ref[:, d * LANES : (d + 1) * LANES]
    heavy = types_ref[...] == 0
    for b in range(PER):
        f = jnp.concatenate(
            [full[d, pl.ds(b, FEATS + 1, stride=PER), :] for d in range(CHUNKS)], 1
        )
        out_ref[b : b + 1, :] = network(f, w1_ref, w2_ref, w3_ref, heavy)


def vmem(count):
    return [pl.BlockSpec(memory_space=pltpu.VMEM)] * count


def params(collective=None):
    if collective is None:
        return pltpu.CompilerParams(vmem_limit_bytes=VMEM_LIMIT)
    return pltpu.CompilerParams(
        vmem_limit_bytes=VMEM_LIMIT, collective_id=collective, has_side_effects=True
    )


def sds(*shape, dtype=F32):
    return jax.ShapeDtypeStruct(shape, dtype)


DMA = pltpu.SemaphoreType.DMA


def propagate(positions, momenta, types, ghost_rows):
    return pl.pallas_call(
        propagate_kernel,
        name="propagate",
        out_shape=(sds(PER, 3, ATOMS), sds(PER, 3, ATOMS), sds(4, 8, TABLE)),
        in_specs=vmem(5),
        out_specs=tuple(vmem(3)),
        scratch_shapes=[
            pltpu.VMEM((8, 3 * ATOMS), F32),
            pltpu.VMEM((64, 3 * LANES), F32),
            pltpu.VMEM((64, 3 * LANES), F32),
            pltpu.VMEM((8, 3 * ATOMS), F32),
            pltpu.VMEM((4, 8, LANES), F32),
            DMA((GROUPS,)),
            DMA((GROUPS,)),
            DMA((GROUPS,)),
            DMA((GROUPS,)),
            DMA((8,)),
            DMA((8,)),
        ],
        compiler_params=params(0),
    )(jnp.asarray(propagator()), positions, momenta, types, ghost_rows)


def features(tab, neighbours, counts, types, w1, w2, w3):
    return pl.pallas_call(
        features_kernel,
        name="features",
        out_shape=(sds(SLOTS, 8, ATOMS), sds(CHUNKS, LANES, LANES), sds(8, ATOMS)),
        in_specs=vmem(7),
        out_specs=tuple(vmem(3)),
        scratch_shapes=[pltpu.VMEM((SLOTS // 2, 8, ATOMS), jnp.int32)],
        compiler_params=params(),
    )(tab, neighbours, counts, types, w1, w2, w3)


def equilibrate(hardness, rhs, coup, neighbours, types, ghost_rows):
    return pl.pallas_call(
        solve_kernel,
        name="equilibrate",
        out_shape=sds(PER, ATOMS),
        in_specs=[pl.BlockSpec(memory_space=pltpu.SMEM)] + vmem(5),
        out_specs=vmem(1)[0],
        scratch_shapes=[
            pltpu.VMEM((SLOTS, 8, ATOMS), jnp.int32),
            pltpu.VMEM((SLOTS, WIDE, ATOMS), BF16),
            pltpu.VMEM((ATOMS, LANES), BF16),
            pltpu.VMEM((8, ATOMS), F32),
            pltpu.VMEM((8, ATOMS), F32),
            pltpu.VMEM((8, ATOMS), F32),
            pltpu.VMEM((8, ATOMS), F32),
            pltpu.VMEM((8, ATOMS), F32),
            pltpu.VMEM((8, TABLE), F32),
            pltpu.VMEM((BLOCKS * BAND, WIDE), F32),
            pltpu.VMEM((9, 8, LANES), F32),
            pltpu.VMEM((1, 8, LANES), F32),
            pltpu.VMEM((9, 8, LANES), F32),
            pltpu.VMEM((2, BRICKS, 8, LANES), F32),
            DMA((8,)),
            DMA((8,)),
            DMA((8,)),
            DMA((8,)),
            DMA((2, BRICKS)),
            DMA((2, BRICKS)),
        ],
        compiler_params=params(1),
    )(hardness, rhs, coup, neighbours, types, ghost_rows)


def final_energies(feats, charges, types, w1, w2, w3):
    return pl.pallas_call(
        energies_kernel,
        name="energies",
        out_shape=sds(PER, ATOMS),
        in_specs=vmem(6),
        out_specs=vmem(1)[0],
        scratch_shapes=[pltpu.VMEM((CHUNKS, LANES, LANES), F32)],
        compiler_params=params(),
    )(feats, charges, types, w1, w2, w3)


def on_device(
    positions,
    momenta,
    types,
    ghost_rows,
    neighbours,
    counts,
    hardness,
    chi_w1,
    chi_w2,
    chi_w3,
    en_w1,
    en_w2,
    en_w3,
):
    types = types.reshape(1, ATOMS)
    counts = counts.reshape(1, ATOMS)
    ghost_rows = ghost_rows.reshape(1, LANES)
    new_positions, new_momenta, tab = propagate(positions, momenta, types, ghost_rows)
    coup, feats, rhs = features(tab, neighbours, counts, types, chi_w1, chi_w2, chi_w3)
    charges = equilibrate(hardness, rhs, coup, neighbours, types, ghost_rows)
    energies = final_energies(feats, charges, types, en_w1, en_w2, en_w3)
    return (new_positions, new_momenta, charges, energies)


def solution(mesh):
    placed = (
        P("bead", None, ("gx", "gy")),
        P("bead", None, ("gx", "gy")),
        P(("gx", "gy")),
        P(("gx", "gy")),
        P(None, ("gx", "gy")),
        P(("gx", "gy")),
        P(),
        P(),
        P(),
        P(),
        P(),
        P(),
        P(),
    )
    return jax.shard_map(
        on_device,
        mesh=mesh,
        in_specs=placed,
        out_specs=(
            P("bead", None, ("gx", "gy")),
            P("bead", None, ("gx", "gy")),
            P("bead", ("gx", "gy")),
            P("bead", ("gx", "gy")),
        ),
        check_vma=False,
    )
```

time: 1990 us -> 132 us (0.07)
  local copies, waits for them, and re-layouts: 924 us -> 7.72 us
  other arithmetic: 556 us -> 0 us
  blocking collectives: 391 us -> 0 us
  Pallas kernels: 0 us -> 123 us
  starting transfers between devices: 80.2 us -> 0 us
  waiting for transfers between devices: 23.5 us -> 0 us
    gather x27 -> x0, local copies, waits for them, and re-layouts: 870 us -> none  [the longest x10 633 us: on_device(): forward = jnp.sum(coupling * value_table[:, :, neighbours], 2)]
    scatter-add x12 -> x0, other arithmetic: 536 us -> none  [the longest x6 527 us: spread_back(): jnp.zeros((layers, atoms + 9 * ghost_count), jnp.float32).at[:, neighbours]]
    psum x10 -> x0, blocking collectives: 376 us -> none  [the longest x5 180 us: residual_sum(): return lax.psum(jnp.sum(residual * residual, -1), ('gx', 'gy'))[..., None]]
    pallas_call x0 -> x4, Pallas kernels: none -> 123 us  [the longest x1 80.3 us: equilibrate(): pl.pallas_call(solve_kernel, name='equilibrate', out_shape=sds(PER, ATOMS...]
    ppermute x48 -> x0, starting transfers between devices: 80.2 us -> none  [the longest x24 59.8 us: with_halo(): lax.ppermute(head, axis, [((i + 1) % count, i) for i in range(count)])]
    mul x11 -> x0, local copies, waits for them, and re-layouts: 23.6 us -> none  [the longest x10 23.4 us: on_device(): coupling[None] * direction[:, :, None, :]]
    ppermute x48 -> x0, waiting for transfers between devices: 23.5 us -> none  [the longest x24 22.2 us: with_halo(): lax.ppermute(tail, axis, [(i, (i + 1) % count) for i in range(count)])]
  transfers between devices with their start and end apart: 48 -> 0, of which waited for: 15 -> 0; matrix products, arithmetic and copies ran while one was open for 61% -> 0% of each run, Pallas kernels for 0% -> 0%
where the time goes in v1:
time: 132 us
  Pallas kernels  123 us (93%)
  local copies, waits for them, and re-layouts  7.72 us (6%)
    pallas_call x1, Pallas kernels, equilibrate(): pl.pallas_call(solve_kernel, name='equilibrate', out_shape=sds(PER, ATOMS...  80.3 us
    pallas_call x1, Pallas kernels, propagate(): pl.pallas_call(propagate_kernel, name='propagate', out_shape=(sds(PER, 3,...  21 us
    pallas_call x1, Pallas kernels, features(): pl.pallas_call(features_kernel, name='features', out_shape=(sds(SLOTS, 8,...  16.5 us
    unnamed x23, local copies, waits for them, and re-layouts  7.72 us
    pallas_call x1, Pallas kernels, final_energies(): pl.pallas_call(energies_kernel, name='energies', out_shape=sds(PER, ATOMS...  5.57 us

profile of v1, /device:TPU:0, one launch (start us, length us, event | category | flops | bytes accessed | tf_op | source)
XLA Modules:
  0.0 131.8 jit_solution(1288097004471244063)
XLA Ops:
  0.6 0.0 copy-start.2
  0.6 1.5 %copy.18.pos_ref = f32[4,3,1024]{2,1,0:T(4,128)} copy(f32[4,3,1024]{2,0,1:T(4,128)} %param.14) | data formatting | bytes 98304 | tf_op args[0]
  2.1 0.0 copy-done.2
  2.1 0.7 copy.19.mom_ref
  2.8 21.0 %propagate.1 = (f32[4,3,1024]{2,1,0:T(4,128)}, f32[4,3,1024]{2,1,0:T(4,128)}, f32[4,8,2176]{2,1,0:T(8,128)}) custom-call(f32[128,64]{1,0:T(8,128)} %constant.2.clone.matrix_ref, f32[4,3,1024]{2,1,0:T(4,128)} %copy.18.pos_ref, f32[4,3,1024]{2,1,0:T(4,128)} %copy.19.mom_ref, s32[1,1024]{1,0:T(1,128)} %bitcast.3, s32[1,128]{1,0:T(1,128)} %bitcast.8), custom_call_target="tpu_custom_call" | custom-call | tf_op jit(solution)/shard_map/propagate/pallas_call | solution.py:567
  23.8 0.0 copy-start.1
  23.8 1.5 %copy.24 = f32[4,3,1024]{2,0,1:T(4,128)} copy(f32[4,3,1024]{2,1,0:T(4,128)} %get-tuple-element.16) | data formatting | bytes 98304
  25.4 0.0 copy-done.1
  25.4 0.0 copy-start.3
  25.4 0.7 copy.25
  26.0 0.1 copy-done.3
  26.1 0.0 copy-start.4
  26.1 0.6 copy.20.w1_ref
  26.7 0.1 copy-done.4
  26.8 0.6 copy.21.w2_ref
  27.5 16.5 %features.1 = (f32[16,8,1024]{2,1,0:T(8,128)}, f32[8,128,128]{2,1,0:T(8,128)}, f32[8,1024]{1,0:T(8,128)}) custom-call(f32[4,8,2176]{2,1,0:T(8,128)} %get-tuple-element.12.tab_ref, s32[16,1024]{1,0:T(8,128)} %idx_ref.3, s32[1,1024]{1,0:T(1,128)} %bitcast.7, s32[1,1024]{1,0:T(1,128)} %bitcast.4, f32[2,25,30]{2,1,0:T(8,128)} %copy.20.w1_ref, ...), custom_call_target="tpu_custom_call" | custom-call | tf_op jit(solution)/shard_map/features/pallas_call | solution.py:591
  43.9 0.0 copy-start.5
  43.9 80.3 %equilibrate.1.charge_ref = f32[4,1024]{1,0:T(4,128)} custom-call(f32[2]{0:T(128)} %hardness_ref.1, f32[8,1024]{1,0:T(8,128)} %get-tuple-element.13.rhs_ref, f32[16,8,1024]{2,1,0:T(8,128)} %get-tuple-element.14.coup_ref, s32[16,1024]{1,0:T(8,128)} %idx_ref.3, s32[1,1024]{1,0:T(1,128)} %bitcast.5, s32[1,128]{1,0:T(1,128)} %bitcast.9), custom_call_target="tpu_custom_call" | custom-call | tf_op jit(solution)/shard_map/equilibrate/pallas_call | solution.py:603
  124.3 0.0 copy-done.5
  124.3 0.0 copy-start.6
  124.3 0.6 copy.22.w1_ref
  124.9 0.1 copy-done.6
  125.0 0.6 copy.23.w2_ref
  125.6 0.0 copy-start
  125.6 5.6 %energies.1 = f32[4,1024]{1,0:T(4,128)} custom-call(f32[8,128,128]{2,1,0:T(8,128)} %get-tuple-element.15.feat_ref, f32[4,1024]{1,0:T(4,128)} %equilibrate.1.charge_ref, s32[1,1024]{1,0:T(1,128)} %bitcast.6, f32[2,25,31]{2,1,0:T(8,128)} %copy.22.w1_ref, f32[2,25,25]{2,1,0:T(8,128)} %copy.23.w2_ref, f32[2,25]{1,0:T(2,128)} %w3_ref.3), custom_call_target="tpu_custom_call" | custom-call | tf_op jit(solution)/shard_map/energies/pallas_call | solution.py:636
  131.2 0.0 copy-done
  131.2 0.6 copy.27
Async XLA Ops:
  0.6 1.5 %copy-start.2 = (f32[4,3,1024]{2,0,1:T(4,128)S(1)}, f32[4,3,1024]{2,0,1:T(4,128)}, u32[]{:S(2)}) copy-start(f32[4,3,1024]{2,0,1:T(4,128)} %param.15) | copy-start | bytes 147460
  23.8 1.5 %copy-start.1 = (f32[4,3,1024]{2,1,0:T(4,128)S(1)}, f32[4,3,1024]{2,1,0:T(4,128)}, u32[]{:S(2)}) copy-start(f32[4,3,1024]{2,1,0:T(4,128)} %get-tuple-element.17) | copy-start | bytes 147460
  25.4 0.7 copy-start.3
  26.1 0.7 copy-start.4
  43.9 80.3 %copy-start.5 = (f32[2,25,31]{2,0,1:T(2,128)S(1)}, f32[2,25,31]{2,0,1:T(2,128)}, u32[]{:S(2)}) copy-start(f32[2,25,31]{2,0,1:T(2,128)} %param.24) | copy-start | bytes 18604
  124.3 0.7 copy-start.6
  125.6 5.6 %copy-start = (f32[4,1024]{1,0:T(4,128)S(1)}, f32[4,1024]{1,0:T(4,128)}, u32[]{:S(2)}) copy-start(f32[4,1024]{1,0:T(4,128)} %equilibrate.1.charge_ref) | copy-start | bytes 49156

commit v2 on v0

v2 whole, which is shorter than its diff:
```python
import functools
import math

import jax
import jax.numpy as jnp
import numpy as np
from jax import lax
from jax.experimental import pallas as pl
from jax.experimental.pallas import tpu as pltpu
from jax.sharding import PartitionSpec as P

MESH = pl.DeviceIdType.MESH
F32 = jnp.float32
BF16 = jnp.bfloat16
HIGHEST = lax.Precision.HIGHEST
ITERS = 5
STEP = 0.5
TOP_FREQ = 80.0
CUTOFF = 4.0
HEAVY_MASS = 16.0
CHI_SCALE = 4.0
LANES = 128
BEADS = 32
GROUPS = 8
PER = 4
ATOMS = 1024
CHUNKS = ATOMS // LANES
SLOTS = 16
TABLE = ATOMS + 8 * LANES
HALF = 15
FEATS = 2 * HALF
SIDE = 4
PAD = 32
BRICKS = SIDE * SIDE
BAND = 16
WIDE = 256
BLOCKS = TABLE // WIDE
OWN_BLOCKS = ATOMS // WIDE
EDGES = SLOTS * ATOMS
GROUP = 4
TOTAL_ATOMS = ATOMS * BRICKS
TINY = 1e-30
SELF = ATOMS + 4 * LANES
VMEM_LIMIT = 60 * 1024 * 1024


def propagator():
    k = np.arange(BEADS)
    omega = TOP_FREQ * np.sin(math.pi * k / BEADS)
    cosine = np.cos(omega * STEP)
    sine = np.sin(omega * STEP)
    drift = np.where(k > 0, TOP_FREQ * sine / np.where(k > 0, omega, 1.0), TOP_FREQ * STEP)
    restoring = -(omega / TOP_FREQ) * sine
    gap = (k[:, None] - k[None, :]) % BEADS

    def spread(weights):
        line = (weights[None, :] * np.cos(2 * math.pi * k[:, None] * k[None, :] / BEADS)).sum(1) / BEADS
        return line[gap]

    keep, push, pull = spread(cosine), spread(drift), spread(restoring)
    zero = np.zeros_like(keep)
    plain = np.block([[keep, zero], [zero, keep]])
    massive = np.block([[zero, push], [pull, zero]])
    order = np.array([half * BEADS + g * PER + b for g in range(GROUPS) for half in range(2) for b in range(PER)])
    both = np.concatenate([plain[order][:, order], massive[order][:, order]], 0)
    return both.astype(np.float32)


def sublanes(shape):
    return lax.broadcasted_iota(jnp.int32, shape, 0)


def lane_take(table, lane):
    return jnp.take_along_axis(table, lane, axis=1, mode="promise_in_bounds")


def row_bits(rows, count):
    return [(rows & (LANES << bit)) != 0 for bit in range(count)]


def pick(parts, bits):
    level = 0
    while len(parts) > 1:
        nxt = [
            jnp.where(bits[level], parts[i + 1], parts[i]) for i in range(0, len(parts) - 1, 2)
        ]
        if len(parts) % 2:
            nxt.append(parts[-1])
        parts = nxt
        level += 1
    return parts[0]


def split(v):
    top = v.astype(BF16).astype(F32)
    return jnp.concatenate([top, v - top], 0).astype(BF16)


def halves(v):
    top = v.astype(BF16)
    return top, (v - top.astype(F32)).astype(BF16)


def lanes_sum(v):
    return jnp.sum(v, axis=1, keepdims=True)


def fold(v, low):
    return jnp.where(low, v, pltpu.roll(v, PER, 0))


def brick_at(dx, dy):
    return {
        "gx": lax.rem(lax.axis_index("gx") + dx + SIDE, SIDE),
        "gy": lax.rem(lax.axis_index("gy") + dy + SIDE, SIDE),
    }


AROUND = [(a, c) for a in range(3) for c in range(3) if (a, c) != (1, 1)]


def load_weights(w1_ref, w2_ref, w3_ref, wide1, wide2, wide3):
    rows, cols = w1_ref.shape[0], w1_ref.shape[2]
    for ref in (wide1, wide2, wide3):
        ref[...] = jnp.zeros_like(ref)
    for e in range(2):
        at = e * PAD
        wide1[at : at + rows, 0:cols] = w1_ref[:, e, :]
        wide2[at : at + rows, at : at + rows] = w2_ref[:, e, :]
        wide3[e : e + 1, at : at + rows] = w3_ref[e : e + 1, :]


def product(w, f):
    w_top, w_rest = halves(w)
    f_top, f_rest = halves(f)
    rows = w.shape[0]
    both = jnp.dot(jnp.concatenate([w_top, w_rest], 0), f_top, preferred_element_type=F32)
    return both[0:rows] + both[rows:] + jnp.dot(w_top, f_rest, preferred_element_type=F32)


def network(feat_ref, wide1, wide2, wide3, heavy):
    f = jnp.concatenate(
        [feat_ref[d, pl.ds(b, PAD, stride=PER), :] for b in range(PER) for d in range(CHUNKS)], 1
    )
    h = jnp.tanh(product(wide1[...], f))
    h = jnp.tanh(product(wide2[...], h))
    out = product(wide3[...], h)
    return [
        jnp.where(
            heavy, out[0:1, b * ATOMS : (b + 1) * ATOMS], out[1:2, b * ATOMS : (b + 1) * ATOMS]
        )
        for b in range(PER)
    ]


def main_kernel(
    hardness_ref,
    matrix_ref,
    pos_ref,
    mom_ref,
    types_ref,
    ghost_ref,
    idx_ref,
    counts_ref,
    w1_ref,
    w2_ref,
    w3_ref,
    newpos_ref,
    newmom_ref,
    charge_ref,
    feat_ref,
    stage,
    modes,
    moved,
    back,
    lent_pos,
    lent_heavy,
    tab,
    idx16,
    heavy16,
    rows_all,
    pairs,
    heavy_pairs,
    block_ids,
    onehot,
    onehot_t,
    ghost_onehot,
    coup,
    coup_own,
    coup_ghost,
    dist,
    weight_h,
    weight_l,
    wide1,
    wide2,
    wide3,
    residual,
    image,
    image2,
    direction,
    steps,
    total,
    degree,
    ghost_table,
    spread,
    lent,
    backin,
    parts,
    send1,
    recv1,
    send2,
    recv2,
    send3,
    recv3,
    send4,
    recv4,
    send_a,
    recv_a,
    send_b,
    recv_b,
    send_d,
    recv_d,
):
    group = lax.axis_index("bead")
    me = lax.axis_index("gx") * SIDE + lax.axis_index("gy")
    others = [(o // SIDE, o % SIDE) for o in range(1, BRICKS)]
    barrier = pltpu.get_barrier_semaphore()
    for o in range(1, GROUPS):
        pl.semaphore_signal(
            barrier, inc=1, device_id={"bead": lax.rem(group + o, GROUPS)}, device_id_type=MESH
        )
    for dx, dy in others:
        pl.semaphore_signal(barrier, inc=1, device_id=brick_at(dx, dy), device_id_type=MESH)

    low = sublanes((8, LANES)) < PER
    low_all = sublanes((8, ATOMS)) < PER
    own_width = 3 * LANES
    width = 2 * own_width
    ghost_rows = jnp.broadcast_to(ghost_ref[...], (8, LANES))
    ghost_lane = ghost_rows & (LANES - 1)
    ghost_bits = row_bits(ghost_rows, 3)

    def at_ghosts(v):
        return pick(
            [lane_take(v[:, d * LANES : (d + 1) * LANES], ghost_lane) for d in range(CHUNKS)],
            ghost_bits,
        )

    heavy_row = types_ref[...] == 0
    heavy = jnp.where(heavy_row, 1.0, 0.0)
    tab[3, :, 0:ATOMS] = jnp.broadcast_to(heavy, (8, ATOMS))
    ghost_heavy = at_ghosts(jnp.broadcast_to(heavy, (8, ATOMS)))
    lent_heavy[...] = ghost_heavy
    for c in range(3):
        v = jnp.concatenate([pos_ref[c], mom_ref[c]], 0)
        g = at_ghosts(v)
        for d in range(CHUNKS):
            at = d * width + c * LANES
            stage[:, at : at + LANES] = v[:, d * LANES : (d + 1) * LANES]
            stage[:, at + own_width : at + own_width + LANES] = g
    pl.semaphore_wait(barrier, GROUPS - 1 + len(others))

    mine = pl.ds(pl.multiple_of(group * 8, 8), 8)
    mine_too = pl.ds(pl.multiple_of(64 + group * 8, 8), 8)
    copies = []
    for o in range(1, GROUPS):
        to = lax.rem(group + o, GROUPS)
        cp = pltpu.make_async_remote_copy(
            src_ref=stage.at[:, pl.ds(pl.multiple_of(to * width, LANES), width)],
            dst_ref=modes.at[mine, :],
            send_sem=send1.at[o],
            recv_sem=recv1.at[o],
            device_id={"bead": to},
            device_id_type=MESH,
        )
        cp.start()
        copies.append(cp)
    heavy_copies = []
    for g, (a, c) in enumerate(AROUND):
        at = ATOMS + g * LANES
        cp = pltpu.make_async_remote_copy(
            src_ref=lent_heavy,
            dst_ref=tab.at[3, :, at : at + LANES],
            send_sem=send4.at[g],
            recv_sem=recv4.at[g],
            device_id=brick_at(1 - a, 1 - c),
            device_id_type=MESH,
        )
        cp.start()
        heavy_copies.append(cp)
    modes[mine, :] = stage[:, pl.ds(pl.multiple_of(group * width, LANES), width)]

    for half in range(2):
        for d in range(CHUNKS):
            lanes = slice(d * LANES, (d + 1) * LANES)
            rows = idx_ref[half * 8 : half * 8 + 8, lanes]
            local = lane_take(ghost_rows, rows & (LANES - 1))
            rows = jnp.where(
                rows < SELF, rows, jnp.where(rows < SELF + LANES, local, rows - LANES)
            )
            idx16[half * 8 : half * 8 + 8, lanes] = rows
    for k in range(SLOTS):
        rows_all[k] = jnp.broadcast_to(idx16[k : k + 1, :], (8, ATOMS))
        block_ids[k] = jnp.broadcast_to(
            (idx16[k : k + 1, :] >> 8).astype(F32), (BAND, ATOMS)
        ).astype(BF16)
    for kp in range(SLOTS // 2):
        pairs[kp] = jnp.where(low_all, rows_all[2 * kp], rows_all[2 * kp + 1])
    within = sublanes((WIDE, ATOMS)).astype(F32).astype(BF16)
    for k in range(SLOTS):
        wide = jnp.broadcast_to((idx16[k : k + 1, :] & (WIDE - 1)).astype(F32), (BAND, ATOMS))
        wide = jnp.concatenate([wide.astype(BF16)] * (WIDE // BAND), 0)
        onehot[:, k * ATOMS : (k + 1) * ATOMS] = jnp.where(within == wide, 1.0, 0.0).astype(BF16)
    for d in range(CHUNKS):
        rows = sublanes((LANES, LANES)) + d * LANES
        hit = rows == jnp.broadcast_to(ghost_ref[...], (LANES, LANES))
        ghost_onehot[d * LANES : (d + 1) * LANES, :] = jnp.where(hit, 1.0, 0.0).astype(BF16)
    load_weights(w1_ref, w2_ref, w3_ref, wide1, wide2, wide3)
    my_types = types_ref[:, pl.ds(pl.multiple_of(group * LANES, LANES), LANES)]
    mass = jnp.broadcast_to(jnp.where(my_types == 0, HEAVY_MASS, 1.0), (8, LANES))
    factor = jnp.concatenate([jnp.where(low, 1.0 / mass, mass)] * 3, 1)
    ghost_mass = jnp.where(ghost_heavy > 0.0, HEAVY_MASS, 1.0)
    ghost_factor = jnp.concatenate([1.0 / ghost_mass] * 3, 1)

    for cp in copies:
        cp.wait()
    ghost_matrix = jnp.concatenate([matrix_ref[mine, :], matrix_ref[mine_too, :]], 0)
    both = jnp.dot(
        ghost_matrix, modes[:, own_width:width], precision=HIGHEST, preferred_element_type=F32
    )
    ghost_pos = both[0:8] + both[8:16] * ghost_factor
    for c in range(3):
        lent_pos[c] = fold(ghost_pos[:, c * LANES : (c + 1) * LANES], low)
    pos_copies = []
    for g, (a, c) in enumerate(AROUND):
        at = ATOMS + g * LANES
        cp = pltpu.make_async_remote_copy(
            src_ref=lent_pos,
            dst_ref=tab.at[0:3, :, at : at + LANES],
            send_sem=send3.at[g],
            recv_sem=recv3.at[g],
            device_id=brick_at(1 - a, 1 - c),
            device_id_type=MESH,
        )
        cp.start()
        pos_copies.append(cp)
    both = jnp.dot(
        matrix_ref[...], modes[:, 0:own_width], precision=HIGHEST, preferred_element_type=F32
    )
    for g in range(GROUPS):
        rows = slice(g * 8, g * 8 + 8)
        moved[rows, :] = both[rows] + both[64 + g * 8 : 72 + g * 8] * factor
    my_lanes = pl.ds(pl.multiple_of(group * own_width, LANES), own_width)
    copies = []
    for o in range(1, GROUPS):
        to = lax.rem(group + o, GROUPS)
        cp = pltpu.make_async_remote_copy(
            src_ref=moved.at[pl.ds(pl.multiple_of(to * 8, 8), 8), :],
            dst_ref=back.at[:, my_lanes],
            send_sem=send2.at[o],
            recv_sem=recv2.at[o],
            device_id={"bead": to},
            device_id_type=MESH,
        )
        cp.start()
        copies.append(cp)
    back[:, my_lanes] = moved[mine, :]

    for cp in heavy_copies:
        cp.wait()
    for half in range(2):
        for d in range(CHUNKS):
            lanes = slice(d * LANES, (d + 1) * LANES)
            rows = idx16[half * 8 : half * 8 + 8, lanes]
            lane = rows & (LANES - 1)
            heavy16[half * 8 : half * 8 + 8, lanes] = pick(
                [
                    lane_take(tab[3, :, t * LANES : (t + 1) * LANES], lane)
                    for t in range(TABLE // LANES)
                ],
                row_bits(rows, 4),
            )
    for kp in range(SLOTS // 2):
        heavy_pairs[kp] = jnp.where(
            low_all,
            jnp.broadcast_to(heavy16[2 * kp : 2 * kp + 1, :], (8, ATOMS)),
            jnp.broadcast_to(heavy16[2 * kp + 1 : 2 * kp + 2, :], (8, ATOMS)),
        )
    for k in range(SLOTS):
        onehot_t[k * ATOMS : (k + 1) * ATOMS, :] = jnp.transpose(
            onehot[:, k * ATOMS : (k + 1) * ATOMS]
        )

    for cp in copies:
        cp.wait()
    for c in range(3):
        for d in range(CHUNKS):
            at = d * own_width + c * LANES
            v = back[:, at : at + LANES]
            newpos_ref[c, :, d * LANES : (d + 1) * LANES] = v[0:PER]
            newmom_ref[c, :, d * LANES : (d + 1) * LANES] = v[PER:8]
            tab[c, :, d * LANES : (d + 1) * LANES] = fold(v, low)
    for cp in pos_copies:
        cp.wait()

    slot_off = jnp.where(low, 0, 1)
    cos_scale = (math.pi / (2.0 * CUTOFF)) ** 2
    cos_terms = [(-1.0) ** n * cos_scale**n / math.factorial(2 * n) for n in range(8)]

    def geometry(ci, carry):
        lanes = pl.ds(pl.multiple_of(ci * LANES, LANES), LANES)
        own = [tab[c, :, lanes] for c in range(3)]
        count = jnp.broadcast_to(counts_ref[:, lanes], (8, LANES))
        for kp in range(SLOTS // 2):
            rows = pairs[kp, :, lanes]
            lane = rows & (LANES - 1)
            bits = row_bits(rows, 4)
            dist_sq = jnp.zeros((8, LANES), F32)
            for c in range(3):
                near = pick(
                    [
                        lane_take(tab[c, :, t * LANES : (t + 1) * LANES], lane)
                        for t in range(TABLE // LANES)
                    ],
                    bits,
                )
                dist_sq = dist_sq + (near - own[c]) ** 2
            close = jnp.minimum(dist_sq, CUTOFF * CUTOFF)
            wave = jnp.full_like(close, cos_terms[-1])
            for term in cos_terms[-2::-1]:
                wave = wave * close + term
            used = ((2 * kp + slot_off) < count) & (dist_sq < CUTOFF * CUTOFF)
            smooth = jnp.where(used, wave * wave, 0.0)
            heavy_w = smooth * heavy_pairs[kp, :, lanes]
            dist[kp, :, lanes] = dist_sq
            weight_h[kp, :, lanes] = heavy_w
            weight_l[kp, :, lanes] = smooth - heavy_w
            coupling = smooth * lax.rsqrt(1.0 + dist_sq)
            turned = pltpu.roll(coupling, PER, 0)
            for k, v in ((2 * kp, jnp.where(low, coupling, turned)), (2 * kp + 1, jnp.where(low, turned, coupling))):
                inside = rows_all[k, :, lanes] < ATOMS
                coup[k, :, lanes] = v
                coup_own[k, :, lanes] = jnp.where(inside, v, 0.0)
                coup_ghost[k, :, lanes] = jnp.where(inside, 0.0, v)
        return carry

    lax.fori_loop(0, CHUNKS, geometry, 0)

    def scatter(terms_of):
        acc = jnp.zeros((BLOCKS * BAND, WIDE), F32)
        for g in range(SLOTS // GROUP):
            tall = []
            for k in range(g * GROUP, (g + 1) * GROUP):
                terms = split(terms_of(k))
                zero = jnp.zeros_like(terms)
                ids = block_ids[k]
                tall.append(
                    jnp.concatenate([jnp.where(ids == b, terms, zero) for b in range(BLOCKS)], 0)
                )
            rows = slice(g * GROUP * ATOMS, (g + 1) * GROUP * ATOMS)
            acc = acc + jnp.dot(
                jnp.concatenate(tall, 1), onehot_t[rows, :], preferred_element_type=F32
            )
        return acc

    def chunk_of(acc, n):
        row, col = (n // 2) * BAND, (n % 2) * LANES
        return acc[row : row + 8, col : col + LANES] + acc[row + 8 : row + 16, col : col + LANES]

    def send_back(acc, par):
        out = []
        for g, (a, c) in enumerate(AROUND):
            spread[par, g] = chunk_of(acc, CHUNKS + g)
        for g, (a, c) in enumerate(AROUND):
            cp = pltpu.make_async_remote_copy(
                src_ref=spread.at[par, g],
                dst_ref=backin.at[par, g],
                send_sem=send_b.at[par, g],
                recv_sem=recv_b.at[par, g],
                device_id=brick_at(a - 1, c - 1),
                device_id_type=MESH,
            )
            cp.start()
            out.append(cp)
        return out

    def own_part(acc):
        return jnp.concatenate([chunk_of(acc, d) for d in range(CHUNKS)], 1)

    def take_back(copies, par):
        for cp in copies:
            cp.wait()
        received = backin[par, 0]
        for g in range(1, len(AROUND)):
            received = received + backin[par, g]
        returned = lax.dot_general(
            split(received), ghost_onehot[...], (((1,), (1,)), ((), ())), preferred_element_type=F32
        )
        return returned[0:8] + returned[8:16]

    def forward(v, weights, acc):
        tall = jnp.concatenate(
            [split(v[:, q * WIDE : (q + 1) * WIDE]) for q in range(OWN_BLOCKS)], 0
        )
        for g in range(SLOTS // GROUP):
            cols = slice(g * GROUP * ATOMS, (g + 1) * GROUP * ATOMS)
            found = jnp.dot(tall, onehot[:, cols], preferred_element_type=F32)
            for kk in range(GROUP):
                k = g * GROUP + kk
                f = found[:, kk * ATOMS : (kk + 1) * ATOMS]
                near = [
                    f[q * BAND : q * BAND + 8] + f[q * BAND + 8 : q * BAND + 16]
                    for q in range(OWN_BLOCKS)
                ]
                rows = rows_all[k]
                acc = acc + weights[k] * pick(near, [(rows & WIDE) != 0, (rows & (2 * WIDE)) != 0])
        return acc

    acc = scatter(lambda k: coup[k])
    first_back = send_back(acc, 1)
    degree[...] = own_part(acc)

    feat_ref[...] = jnp.zeros_like(feat_ref)

    def radial(ci, carry):
        lanes = pl.ds(pl.multiple_of(ci * LANES, LANES), LANES)
        sums = [jnp.zeros((8, LANES), F32) for _ in range(FEATS)]
        for kp in range(SLOTS // 2):
            d = dist[kp, :, lanes]
            wh = weight_h[kp, :, lanes]
            wl = weight_l[kp, :, lanes]
            for s in range(HALF):
                eta = 0.2 * 20.0 ** (s / (HALF - 1))
                falloff = jnp.exp(d * (-eta))
                sums[s] = sums[s] + wh * falloff
                sums[HALF + s] = sums[HALF + s] + wl * falloff
        for s in range(FEATS):
            v = jnp.log(1.0 + (sums[s] + pltpu.roll(sums[s], PER, 0)))
            feat_ref[ci, s * PER : (s + 1) * PER, :] = v[0:PER]
        return carry

    lax.fori_loop(0, CHUNKS, radial, 0)
    for b, chi in enumerate(network(feat_ref, wide1, wide2, wide3, heavy_row)):
        residual[b : b + 1, :] = -CHI_SCALE * chi
    residual[PER:8, :] = jnp.broadcast_to(1.0 - heavy, (PER, ATOMS))
    around = degree[...] + take_back(first_back, 1)
    for k in range(SLOTS):
        around = around + coup[k]
    h0, h1 = hardness_ref[0], hardness_ref[1]
    hard = jnp.where(heavy_row, h0, h1)
    degree[...] = hard + 0.5 * around

    def apply(ref, par, dots):
        lent[par] = at_ghosts(ref[...])
        first = []
        for g, (a, c) in enumerate(AROUND):
            cp = pltpu.make_async_remote_copy(
                src_ref=lent.at[par],
                dst_ref=ghost_table.at[par, :, g * LANES : (g + 1) * LANES],
                send_sem=send_a.at[par, g],
                recv_sem=recv_a.at[par, g],
                device_id=brick_at(1 - a, 1 - c),
                device_id_type=MESH,
            )
            cp.start()
            first.append(cp)
        third = send_dots(par) if dots else []
        acc = scatter(lambda k: coup[k] * ref[...])
        second = send_back(acc, par)
        around = forward(ref[...], coup_own, own_part(acc))
        for cp in first:
            cp.wait()
        around = forward(ghost_table[par], coup_ghost, around)
        around = around + take_back(second, par)
        return degree[...] * ref[...] - 0.5 * around, third

    lane_id = lax.broadcasted_iota(jnp.int32, (8, LANES), 1)

    def send_dots(par):
        r = residual[...]
        dots = [lanes_sum(r * r), lanes_sum(r * image[...]), lanes_sum(r * steps[...]), lanes_sum(r)]
        v = dots[3]
        for n in (2, 1, 0):
            v = jnp.where(lane_id == n, dots[n], v)
        parts[par, me] = v
        out = []
        for n, (dx, dy) in enumerate(others):
            cp = pltpu.make_async_remote_copy(
                src_ref=parts.at[par, me],
                dst_ref=parts.at[par, me],
                send_sem=send_d.at[par, n],
                recv_sem=recv_d.at[par, n],
                device_id=brick_at(dx, dy),
                device_id_type=MESH,
            )
            cp.start()
            out.append(cp)
        return out

    def take_dots(copies, par):
        for cp in copies:
            cp.wait()
        whole = parts[par, 0]
        for n in range(1, BRICKS):
            whole = whole + parts[par, n]
        return [whole[:, n : n + 1] for n in range(4)]

    alpha_max = 2.0 / jnp.minimum(h0, h1)

    def step_sizes(dots, state, start):
        norm, rw, rs, r_sum = dots
        norm_prev, curve_prev, sum_prev, sum_total = state
        beta = jnp.where(start, 0.0, norm / jnp.maximum(norm_prev, TINY))
        curve = rw + 2.0 * beta * rs + beta * beta * curve_prev
        alpha = jnp.minimum(norm / jnp.maximum(curve, TINY), alpha_max)
        p_sum = r_sum + beta * sum_prev
        return alpha, beta, (norm, curve, p_sum, sum_total + alpha * p_sum)

    image[...] = apply(residual, 0, False)[0]
    for ref in (direction, steps, image2, total):
        ref[...] = jnp.zeros_like(ref)
    high = jnp.logical_not(low_all)
    high_col = sublanes((8, 1)) >= PER

    def sweep(it, state):
        par = lax.rem(it + 1, 2)
        start = it == 0
        q, third = apply(image, par, True)
        dots = take_dots(third, par)
        light = dots[3]
        alpha, beta, state = step_sizes(dots, state, start)
        r, w = residual[...], image[...]
        z = q + beta * image2[...]
        s = w + beta * steps[...]
        p = r + beta * direction[...]
        x = total[...] + alpha * p
        r_new = r - alpha * s
        w_new = w - alpha * z
        known = jnp.logical_and(start, high)
        gap = h1 - h0
        hard_sum = (TOTAL_ATOMS - light) * h0 + light * h1
        c0 = light / hard_sum
        c1 = -TOTAL_ATOMS / hard_sum
        direction[...] = jnp.where(known, 1.0, p)
        steps[...] = jnp.where(known, hard, s)
        image2[...] = jnp.where(known, h0 * hard + gap * w, z)
        total[...] = jnp.where(known, TOTAL_ATOMS / hard_sum, x)
        residual[...] = jnp.where(known, gap * (c0 + c1 * r), r_new)
        image[...] = jnp.where(known, gap * (c0 * hard + c1 * w), w_new)
        exact = (
            jnp.full((8, 1), TOTAL_ATOMS, F32),
            hard_sum,
            jnp.full((8, 1), TOTAL_ATOMS, F32),
            TOTAL_ATOMS / hard_sum * TOTAL_ATOMS,
        )
        known_col = jnp.logical_and(start, high_col)
        return tuple(jnp.where(known_col, e, v) for e, v in zip(exact, state))

    zero = jnp.zeros((8, 1), F32)
    state = lax.fori_loop(0, ITERS - 1, sweep, (zero + 1.0, zero, zero, zero))
    par = ITERS % 2
    dots = take_dots(send_dots(par), par)
    alpha, beta, state = step_sizes(dots, state, False)
    x = total[...] + alpha * (residual[...] + beta * direction[...])
    sums = state[3]
    charge_ref[...] = x[0:PER] - (sums[0:PER] / sums[PER:8]) * x[PER:8]


def energies_kernel(
    feat_ref,
    charge_ref,
    newpos_ref,
    newmom_ref,
    types_ref,
    w1_ref,
    w2_ref,
    w3_ref,
    pos_out,
    mom_out,
    charge_out,
    out_ref,
    full,
    wide1,
    wide2,
    wide3,
):
    pos_out[...] = newpos_ref[...]
    mom_out[...] = newmom_ref[...]
    charge_out[...] = charge_ref[...]
    load_weights(w1_ref, w2_ref, w3_ref, wide1, wide2, wide3)
    full[...] = feat_ref[...]
    for d in range(CHUNKS):
        full[d, FEATS * PER : (FEATS + 1) * PER, :] = charge_ref[:, d * LANES : (d + 1) * LANES]
    for b, e in enumerate(network(full, wide1, wide2, wide3, types_ref[...] == 0)):
        out_ref[b : b + 1, :] = e


def vmem(count):
    return [pl.BlockSpec(memory_space=pltpu.VMEM)] * count


def sds(*shape, dtype=F32):
    return jax.ShapeDtypeStruct(shape, dtype)


def f32(*shape):
    return pltpu.VMEM(shape, F32)


def on_device(
    positions,
    momenta,
    types,
    ghost_rows,
    neighbours,
    counts,
    hardness,
    chi_w1,
    chi_w2,
    chi_w3,
    en_w1,
    en_w2,
    en_w3,
):
    types = types.reshape(1, ATOMS)
    counts = counts.reshape(1, ATOMS)
    ghost_rows = ghost_rows.reshape(1, LANES)
    turn = lambda v: jnp.transpose(v, (1, 0, 2))
    dma = pltpu.SemaphoreType.DMA
    i32 = jnp.int32
    networks = [f32(2 * PAD, PAD), f32(2 * PAD, 2 * PAD), f32(8, 2 * PAD)]
    new_pos, new_mom, charges, feats = pl.pallas_call(
        main_kernel,
        name="main",
        out_shape=(
            sds(3, PER, ATOMS),
            sds(3, PER, ATOMS),
            sds(PER, ATOMS),
            sds(CHUNKS, LANES, LANES),
        ),
        in_specs=[pl.BlockSpec(memory_space=pltpu.SMEM)] + vmem(10),
        out_specs=tuple(vmem(4)),
        scratch_shapes=[
            f32(8, 6 * ATOMS),
            f32(64, 6 * LANES),
            f32(64, 3 * LANES),
            f32(8, 3 * ATOMS),
            f32(3, 8, LANES),
            f32(8, LANES),
            f32(4, 8, TABLE),
            pltpu.VMEM((SLOTS, ATOMS), i32),
            f32(SLOTS, ATOMS),
            pltpu.VMEM((SLOTS, 8, ATOMS), i32),
            pltpu.VMEM((SLOTS // 2, 8, ATOMS), i32),
            f32(SLOTS // 2, 8, ATOMS),
            pltpu.VMEM((SLOTS, BAND, ATOMS), BF16),
            pltpu.VMEM((WIDE, EDGES), BF16),
            pltpu.VMEM((EDGES, WIDE), BF16),
            pltpu.VMEM((ATOMS, LANES), BF16),
            f32(SLOTS, 8, ATOMS),
            f32(SLOTS, 8, ATOMS),
            f32(SLOTS, 8, ATOMS),
            f32(SLOTS // 2, 8, ATOMS),
            f32(SLOTS // 2, 8, ATOMS),
            f32(SLOTS // 2, 8, ATOMS),
            *networks,
            *[f32(8, ATOMS) for _ in range(7)],
            f32(2, 8, ATOMS),
            f32(2, 8, 8, LANES),
            f32(2, 8, LANES),
            f32(2, 8, 8, LANES),
            f32(2, BRICKS, 8, LANES),
            *[dma((GROUPS,)) for _ in range(4)],
            *[dma((8,)) for _ in range(4)],
            *[dma((2, 8)) for _ in range(4)],
            *[dma((2, BRICKS)) for _ in range(2)],
        ],
        compiler_params=pltpu.CompilerParams(
            vmem_limit_bytes=VMEM_LIMIT, collective_id=0, has_side_effects=True
        ),
    )(
        hardness,
        jnp.asarray(propagator()),
        turn(positions),
        turn(momenta),
        types,
        ghost_rows,
        neighbours,
        counts,
        turn(chi_w1),
        turn(chi_w2),
        chi_w3,
    )
    new_pos, new_mom, charges, energies = pl.pallas_call(
        energies_kernel,
        name="energies",
        out_shape=(sds(3, PER, ATOMS), sds(3, PER, ATOMS), sds(PER, ATOMS), sds(PER, ATOMS)),
        in_specs=vmem(8),
        out_specs=tuple(vmem(4)),
        scratch_shapes=[f32(CHUNKS, LANES, LANES), *networks],
        compiler_params=pltpu.CompilerParams(vmem_limit_bytes=VMEM_LIMIT),
    )(feats, charges, new_pos, new_mom, types, turn(en_w1), turn(en_w2), en_w3)
    return (turn(new_pos), turn(new_mom), charges, energies)


def solution(mesh):
    placed = (
        P("bead", None, ("gx", "gy")),
        P("bead", None, ("gx", "gy")),
        P(("gx", "gy")),
        P(("gx", "gy")),
        P(None, ("gx", "gy")),
        P(("gx", "gy")),
        P(),
        P(),
        P(),
        P(),
        P(),
        P(),
        P(),
    )
    return jax.shard_map(
        on_device,
        mesh=mesh,
        in_specs=placed,
        out_specs=(
            P("bead", None, ("gx", "gy")),
            P("bead", None, ("gx", "gy")),
            P("bead", ("gx", "gy")),
            P("bead", ("gx", "gy")),
        ),
        check_vma=False,
    )
```

time: 1990 us -> 78.1 us (0.04)
  local copies, waits for them, and re-layouts: 924 us -> 0 us
  other arithmetic: 556 us -> 0 us
  blocking collectives: 391 us -> 0 us
  starting transfers between devices: 80.2 us -> 0 us
  Pallas kernels: 0 us -> 77.3 us
  waiting for transfers between devices: 23.5 us -> 0 us
    gather x27 -> x0, local copies, waits for them, and re-layouts: 870 us -> none  [the longest x10 633 us: on_device(): forward = jnp.sum(coupling * value_table[:, :, neighbours], 2)]
    scatter-add x12 -> x0, other arithmetic: 536 us -> none  [the longest x6 527 us: spread_back(): jnp.zeros((layers, atoms + 9 * ghost_count), jnp.float32).at[:, neighbours]]
    psum x10 -> x0, blocking collectives: 376 us -> none  [the longest x5 180 us: residual_sum(): return lax.psum(jnp.sum(residual * residual, -1), ('gx', 'gy'))[..., None]]
    ppermute x48 -> x0, starting transfers between devices: 80.2 us -> none  [the longest x24 59.8 us: with_halo(): lax.ppermute(head, axis, [((i + 1) % count, i) for i in range(count)])]
    pallas_call x0 -> x2, Pallas kernels: none -> 77.3 us  [the longest x1 74.3 us: on_device(): pl.pallas_call(main_kernel, name='main', out_shape=(sds(3, PER, ATOMS), s...]
    mul x11 -> x0, local copies, waits for them, and re-layouts: 23.6 us -> none  [the longest x10 23.4 us: on_device(): coupling[None] * direction[:, :, None, :]]
    ppermute x48 -> x0, waiting for transfers between devices: 23.5 us -> none  [the longest x24 22.2 us: with_halo(): lax.ppermute(tail, axis, [(i, (i + 1) % count) for i in range(count)])]
  transfers between devices with their start and end apart: 48 -> 0, of which waited for: 15 -> 0; matrix products, arithmetic and copies ran while one was open for 61% -> 0% of each run, Pallas kernels for 0% -> 0%
where the time goes in v2:
time: 78.1 us; the launch traced here: 77.9 us
  Pallas kernels  77.3 us (99%)
    pallas_call x1, Pallas kernels, on_device(): pl.pallas_call(main_kernel, name='main', out_shape=(sds(3, PER, ATOMS), s...  74.3 us
    pallas_call x1, Pallas kernels, on_device(): pl.pallas_call(energies_kernel, name='energies', out_shape=(sds(3, PER, A...  2.94 us

profile of v2, /device:TPU:0, one launch (start us, length us, event | category | flops | bytes accessed | tf_op | source)
XLA Modules:
  0.0 77.9 jit_solution(3680230958334818676)
XLA Ops:
  0.6 74.3 %main.1 = (f32[3,4,1024]{2,1,0:T(4,128)}, f32[3,4,1024]{2,1,0:T(4,128)}, f32[4,1024]{1,0:T(4,128)}, f32[8,128,128]{2,1,0:T(8,128)}) custom-call(f32[2]{0:T(128)} %hardness_ref.1, f32[128,64]{1,0:T(8,128)} %constant.2.clone.matrix_ref, f32[3,4,1024]{2,1,0:T(4,128)} %bitcast.11, f32[3,4,1024]{2,1,0:T(4,128)} %bitcast.12, s32[1,1024]{1,0:T(1,128)} %bitcast.17, ...), custom_call_target="tpu_custom_call" | custom-call | tf_op jit(solution)/shard_map/main/pallas_call | solution.py:732
  75.0 2.9 %energies.1 = (f32[3,4,1024]{2,1,0:T(4,128)}, f32[3,4,1024]{2,1,0:T(4,128)}, f32[4,1024]{1,0:T(4,128)}, f32[4,1024]{1,0:T(4,128)}) custom-call(f32[8,128,128]{2,1,0:T(8,128)} %get-tuple-element.12.feat_ref, f32[4,1024]{1,0:T(4,128)} %get-tuple-element.13.charge_ref, f32[3,4,1024]{2,1,0:T(4,128)} %get-tuple-element.14.newpos_ref, ...), custom_call_target="tpu_custom_call" | custom-call | tf_op jit(solution)/shard_map/energies/pallas_call | solution.py:794

commit v3 on v2

--- a/solution.py
+++ b/solution.py
@@ -138,12 +138,14 @@
     return both[0:rows] + both[rows:] + jnp.dot(w_top, f_rest, preferred_element_type=F32)
 
 
-def network(feat_ref, wide1, wide2, wide3, heavy):
-    f = jnp.concatenate(
+def features_of(feat_ref):
+    return jnp.concatenate(
         [feat_ref[d, pl.ds(b, PAD, stride=PER), :] for b in range(PER) for d in range(CHUNKS)], 1
     )
-    h = jnp.tanh(product(wide1[...], f))
-    h = jnp.tanh(product(wide2[...], h))
+
+
+def network(hidden, wide2, wide3, heavy):
+    h = jnp.tanh(product(wide2[...], jnp.tanh(hidden)))
     out = product(wide3[...], h)
     return [
         jnp.where(
@@ -154,6 +156,24 @@
 
 
 def main_kernel(
+    hardness_hbm,
+    matrix_hbm,
+    pos_hbm,
+    mom_hbm,
+    types_hbm,
+    ghost_hbm,
+    idx_hbm,
+    counts_hbm,
+    w1_hbm,
+    w2_hbm,
+    w3_hbm,
+    v1_hbm,
+    v2_hbm,
+    v3_hbm,
+    newpos_hbm,
+    newmom_hbm,
+    charge_hbm,
+    energy_hbm,
     hardness_ref,
     matrix_ref,
     pos_ref,
@@ -165,9 +185,13 @@
     w1_ref,
     w2_ref,
     w3_ref,
+    v1_ref,
+    v2_ref,
+    v3_ref,
     newpos_ref,
     newmom_ref,
     charge_ref,
+    energy_ref,
     feat_ref,
     stage,
     modes,
@@ -186,14 +210,16 @@
     onehot_t,
     ghost_onehot,
     coup,
-    coup_own,
-    coup_ghost,
     dist,
     weight_h,
     weight_l,
     wide1,
     wide2,
     wide3,
+    last1,
+    last2,
+    last3,
+    first_layer,
     residual,
     image,
     image2,
@@ -201,9 +227,9 @@
     steps,
     total,
     degree,
-    ghost_table,
     spread,
     lent,
+    ghost_in,
     backin,
     parts,
     send1,
@@ -220,6 +246,8 @@
     recv_b,
     send_d,
     recv_d,
+    loads,
+    stores,
 ):
     group = lax.axis_index("bead")
     me = lax.axis_index("gx") * SIDE + lax.axis_index("gy")
@@ -229,8 +257,33 @@
         pl.semaphore_signal(
             barrier, inc=1, device_id={"bead": lax.rem(group + o, GROUPS)}, device_id_type=MESH
         )
-    for dx, dy in others:
-        pl.semaphore_signal(barrier, inc=1, device_id=brick_at(dx, dy), device_id_type=MESH)
+    for a, c in AROUND:
+        pl.semaphore_signal(barrier, inc=1, device_id=brick_at(a - 1, c - 1), device_id_type=MESH)
+    loading = [
+        pltpu.make_async_copy(src, dst, loads.at[n])
+        for n, (src, dst) in enumerate(
+            (
+                (pos_hbm, pos_ref),
+                (mom_hbm, mom_ref),
+                (ghost_hbm, ghost_ref),
+                (types_hbm, types_ref),
+                (idx_hbm, idx_ref),
+                (matrix_hbm, matrix_ref),
+                (counts_hbm, counts_ref),
+                (hardness_hbm, hardness_ref),
+                (w1_hbm, w1_ref),
+                (w2_hbm, w2_ref),
+                (w3_hbm, w3_ref),
+                (v1_hbm, v1_ref),
+                (v2_hbm, v2_ref),
+                (v3_hbm, v3_ref),
+            )
+        )
+    ]
+    for cp in loading:
+        cp.start()
+    for cp in loading[0:4]:
+        cp.wait()
 
     low = sublanes((8, LANES)) < PER
     low_all = sublanes((8, ATOMS)) < PER
@@ -258,7 +311,7 @@
             at = d * width + c * LANES
             stage[:, at : at + LANES] = v[:, d * LANES : (d + 1) * LANES]
             stage[:, at + own_width : at + own_width + LANES] = g
-    pl.semaphore_wait(barrier, GROUPS - 1 + len(others))
+    pl.semaphore_wait(barrier, GROUPS - 1 + len(AROUND))
 
     mine = pl.ds(pl.multiple_of(group * 8, 8), 8)
     mine_too = pl.ds(pl.multiple_of(64 + group * 8, 8), 8)
@@ -290,6 +343,8 @@
         heavy_copies.append(cp)
     modes[mine, :] = stage[:, pl.ds(pl.multiple_of(group * width, LANES), width)]
 
+    for cp in loading[4:]:
+        cp.wait()
     for half in range(2):
         for d in range(CHUNKS):
             lanes = slice(d * LANES, (d + 1) * LANES)
@@ -311,11 +366,8 @@
         wide = jnp.broadcast_to((idx16[k : k + 1, :] & (WIDE - 1)).astype(F32), (BAND, ATOMS))
         wide = jnp.concatenate([wide.astype(BF16)] * (WIDE // BAND), 0)
         onehot[:, k * ATOMS : (k + 1) * ATOMS] = jnp.where(within == wide, 1.0, 0.0).astype(BF16)
-    for d in range(CHUNKS):
-        rows = sublanes((LANES, LANES)) + d * LANES
-        hit = rows == jnp.broadcast_to(ghost_ref[...], (LANES, LANES))
-        ghost_onehot[d * LANES : (d + 1) * LANES, :] = jnp.where(hit, 1.0, 0.0).astype(BF16)
     load_weights(w1_ref, w2_ref, w3_ref, wide1, wide2, wide3)
+    load_weights(v1_ref, v2_ref, v3_ref, last1, last2, last3)
     my_types = types_ref[:, pl.ds(pl.multiple_of(group * LANES, LANES), LANES)]
     mass = jnp.broadcast_to(jnp.where(my_types == 0, HEAVY_MASS, 1.0), (8, LANES))
     factor = jnp.concatenate([jnp.where(low, 1.0 / mass, mass)] * 3, 1)
@@ -366,6 +418,11 @@
         copies.append(cp)
     back[:, my_lanes] = moved[mine, :]
 
+    for d in range(CHUNKS):
+        rows = sublanes((LANES, LANES)) + d * LANES
+        hit = rows == jnp.broadcast_to(ghost_ref[...], (LANES, LANES))
+        hit = jnp.where(hit, 1.0, 0.0).astype(BF16)
+        ghost_onehot[:, d * LANES : (d + 1) * LANES] = jnp.transpose(hit)
     for cp in heavy_copies:
         cp.wait()
     for half in range(2):
@@ -400,6 +457,12 @@
             newpos_ref[c, :, d * LANES : (d + 1) * LANES] = v[0:PER]
             newmom_ref[c, :, d * LANES : (d + 1) * LANES] = v[PER:8]
             tab[c, :, d * LANES : (d + 1) * LANES] = fold(v, low)
+    storing = [
+        pltpu.make_async_copy(newpos_ref, newpos_hbm, stores.at[0]),
+        pltpu.make_async_copy(newmom_ref, newmom_hbm, stores.at[1]),
+    ]
+    for cp in storing:
+        cp.start()
     for cp in pos_copies:
         cp.wait()
 
@@ -438,17 +501,16 @@
             coupling = smooth * lax.rsqrt(1.0 + dist_sq)
             turned = pltpu.roll(coupling, PER, 0)
             for k, v in ((2 * kp, jnp.where(low, coupling, turned)), (2 * kp + 1, jnp.where(low, turned, coupling))):
-                inside = rows_all[k, :, lanes] < ATOMS
                 coup[k, :, lanes] = v
-                coup_own[k, :, lanes] = jnp.where(inside, v, 0.0)
-                coup_ghost[k, :, lanes] = jnp.where(inside, 0.0, v)
         return carry
 
     lax.fori_loop(0, CHUNKS, geometry, 0)
 
-    def scatter(terms_of):
+    def scatter(terms_of, beside=None):
         acc = jnp.zeros((BLOCKS * BAND, WIDE), F32)
         for g in range(SLOTS // GROUP):
+            if beside is not None:
+                beside(g)
             tall = []
             for k in range(g * GROUP, (g + 1) * GROUP):
                 terms = split(terms_of(k))
@@ -494,97 +556,124 @@
         for g in range(1, len(AROUND)):
             received = received + backin[par, g]
         returned = lax.dot_general(
-            split(received), ghost_onehot[...], (((1,), (1,)), ((), ())), preferred_element_type=F32
+            split(received), ghost_onehot[...], (((1,), (0,)), ((), ())), preferred_element_type=F32
         )
         return returned[0:8] + returned[8:16]
 
-    def forward(v, weights, acc):
-        tall = jnp.concatenate(
-            [split(v[:, q * WIDE : (q + 1) * WIDE]) for q in range(OWN_BLOCKS)], 0
-        )
+    def blocks_of(pieces):
+        return jnp.concatenate([split(v) for v in pieces], 0)
+
+    def by_product(tall, g, inside, acc):
+        cols = slice(g * GROUP * ATOMS, (g + 1) * GROUP * ATOMS)
+        found = jnp.dot(tall, onehot[:, cols], preferred_element_type=F32)
+        for kk in range(GROUP):
+            k = g * GROUP + kk
+            f = found[:, kk * ATOMS : (kk + 1) * ATOMS]
+            near = [
+                f[q * BAND : q * BAND + 8] + f[q * BAND + 8 : q * BAND + 16]
+                for q in range(OWN_BLOCKS)
+            ]
+            rows = rows_all[k]
+            near = pick(near, [(rows & WIDE) != 0, (rows & (2 * WIDE)) != 0])
+            hit = (rows < ATOMS) if inside else (rows >= ATOMS)
+            acc = acc + jnp.where(hit, coup[k], 0.0) * near
+        return acc
+
+    def by_lookup(chunks, g, acc):
+        out = []
+        for d in range(CHUNKS):
+            lanes = slice(d * LANES, (d + 1) * LANES)
+            v = acc[:, lanes]
+            for k in range(g * GROUP, (g + 1) * GROUP):
+                rows = rows_all[k, :, lanes]
+                lane = rows & (LANES - 1)
+                near = pick([lane_take(t, lane) for t in chunks], row_bits(rows, 3))
+                v = v + jnp.where(rows >= ATOMS, coup[k, :, lanes], 0.0) * near
+            out.append(v)
+        return jnp.concatenate(out, 1)
+
+    def forward_own(v, acc):
+        tall = blocks_of([v[:, q * WIDE : (q + 1) * WIDE] for q in range(OWN_BLOCKS)])
         for g in range(SLOTS // GROUP):
-            cols = slice(g * GROUP * ATOMS, (g + 1) * GROUP * ATOMS)
-            found = jnp.dot(tall, onehot[:, cols], preferred_element_type=F32)
-            for kk in range(GROUP):
-                k = g * GROUP + kk
-                f = found[:, kk * ATOMS : (kk + 1) * ATOMS]
-                near = [
-                    f[q * BAND : q * BAND + 8] + f[q * BAND + 8 : q * BAND + 16]
-                    for q in range(OWN_BLOCKS)
-                ]
-                rows = rows_all[k]
-                acc = acc + weights[k] * pick(near, [(rows & WIDE) != 0, (rows & (2 * WIDE)) != 0])
+            acc = by_product(tall, g, True, acc)
         return acc
 
-    acc = scatter(lambda k: coup[k])
-    first_back = send_back(acc, 1)
-    degree[...] = own_part(acc)
+    def forward_ghosts(par, acc):
+        chunks = [ghost_in[par, t] for t in range(len(AROUND))]
+        tall = blocks_of(
+            [jnp.concatenate(chunks[2 * q : 2 * q + 2], 1) for q in range(OWN_BLOCKS)]
+        )
+        half = SLOTS // GROUP // 2
+        for g in range(half):
+            acc = by_product(tall, g, False, acc)
+            acc = by_lookup(chunks, half + g, acc)
+        return acc
 
     feat_ref[...] = jnp.zeros_like(feat_ref)
 
-    def radial(ci, carry):
-        lanes = pl.ds(pl.multiple_of(ci * LANES, LANES), LANES)
+    def radial(ci):
+        lanes = slice(ci * LANES, (ci + 1) * LANES)
         sums = [jnp.zeros((8, LANES), F32) for _ in range(FEATS)]
         for kp in range(SLOTS // 2):
             d = dist[kp, :, lanes]
             wh = weight_h[kp, :, lanes]
             wl = weight_l[kp, :, lanes]
             for s in range(HALF):
-                eta = 0.2 * 20.0 ** (s / (HALF - 1))
-                falloff = jnp.exp(d * (-eta))
+                rate = -0.2 * 20.0 ** (s / (HALF - 1)) * math.log2(math.e)
+                falloff = jnp.exp2(d * rate)
                 sums[s] = sums[s] + wh * falloff
                 sums[HALF + s] = sums[HALF + s] + wl * falloff
         for s in range(FEATS):
             v = jnp.log(1.0 + (sums[s] + pltpu.roll(sums[s], PER, 0)))
             feat_ref[ci, s * PER : (s + 1) * PER, :] = v[0:PER]
-        return carry
-
-    lax.fori_loop(0, CHUNKS, radial, 0)
-    for b, chi in enumerate(network(feat_ref, wide1, wide2, wide3, heavy_row)):
+
+    def radial_pair(g):
+        radial(2 * g)
+        radial(2 * g + 1)
+
+    acc = scatter(lambda k: coup[k], radial_pair)
+    first_back = send_back(acc, 2)
+    around = own_part(acc)
+    for k in range(SLOTS):
+        around = around + coup[k]
+    degree[...] = around
+
+    hidden = product(wide1[...], features_of(feat_ref))
+    for b, chi in enumerate(network(hidden, wide2, wide3, heavy_row)):
         residual[b : b + 1, :] = -CHI_SCALE * chi
     residual[PER:8, :] = jnp.broadcast_to(1.0 - heavy, (PER, ATOMS))
-    around = degree[...] + take_back(first_back, 1)
-    for k in range(SLOTS):
-        around = around + coup[k]
     h0, h1 = hardness_ref[0], hardness_ref[1]
     hard = jnp.where(heavy_row, h0, h1)
-    degree[...] = hard + 0.5 * around
-
-    def apply(ref, par, dots):
+
+    lane_id = lax.broadcasted_iota(jnp.int32, (8, LANES), 1)
+
+    def dots_of(r):
+        dots = [lanes_sum(r * r), lanes_sum(r * image[...]), lanes_sum(r * steps[...]), lanes_sum(r)]
+        v = dots[3]
+        for n in (2, 1, 0):
+            v = jnp.where(lane_id == n, dots[n], v)
+        return v
+
+    def send_lent(ref, par):
         lent[par] = at_ghosts(ref[...])
-        first = []
+        out = []
         for g, (a, c) in enumerate(AROUND):
             cp = pltpu.make_async_remote_copy(
                 src_ref=lent.at[par],
-                dst_ref=ghost_table.at[par, :, g * LANES : (g + 1) * LANES],
+                dst_ref=ghost_in.at[par, g],
                 send_sem=send_a.at[par, g],
                 recv_sem=recv_a.at[par, g],
                 device_id=brick_at(1 - a, 1 - c),
                 device_id_type=MESH,
             )
             cp.start()
-            first.append(cp)
-        third = send_dots(par) if dots else []
-        acc = scatter(lambda k: coup[k] * ref[...])
-        second = send_back(acc, par)
-        around = forward(ref[...], coup_own, own_part(acc))
-        for cp in first:
-            cp.wait()
-        around = forward(ghost_table[par], coup_ghost, around)
-        around = around + take_back(second, par)
-        return degree[...] * ref[...] - 0.5 * around, third
-
-    lane_id = lax.broadcasted_iota(jnp.int32, (8, LANES), 1)
-
-    def send_dots(par):
-        r = residual[...]
-        dots = [lanes_sum(r * r), lanes_sum(r * image[...]), lanes_sum(r * steps[...]), lanes_sum(r)]
-        v = dots[3]
-        for n in (2, 1, 0):
-            v = jnp.where(lane_id == n, dots[n], v)
-        parts[par, me] = v
+            out.append(cp)
+        return out
+
+    def send_dots(par, targets):
         out = []
-        for n, (dx, dy) in enumerate(others):
+        for dx, dy in targets:
+            n = dx * SIDE + dy
             cp = pltpu.make_async_remote_copy(
                 src_ref=parts.at[par, me],
                 dst_ref=parts.at[par, me],
@@ -616,7 +705,16 @@
         p_sum = r_sum + beta * sum_prev
         return alpha, beta, (norm, curve, p_sum, sum_total + alpha * p_sum)
 
-    image[...] = apply(residual, 0, False)[0]
+    copies = send_lent(residual, 0)
+    acc = scatter(lambda k: coup[k] * residual[...])
+    second = send_back(acc, 0)
+    around = forward_own(residual[...], own_part(acc))
+    deg = hard + 0.5 * (degree[...] + take_back(first_back, 2))
+    degree[...] = deg
+    for cp in copies:
+        cp.wait()
+    around = forward_ghosts(0, around)
+    image[...] = deg * residual[...] - 0.5 * (around + take_back(second, 0))
     for ref in (direction, steps, image2, total):
         ref[...] = jnp.zeros_like(ref)
     high = jnp.logical_not(low_all)
@@ -625,11 +723,20 @@
     def sweep(it, state):
         par = lax.rem(it + 1, 2)
         start = it == 0
-        q, third = apply(image, par, True)
+        r, w = residual[...], image[...]
+        first = send_lent(image, par)
+        parts[par, me] = dots_of(r)
+        third = send_dots(par, others)
+        acc = scatter(lambda k: coup[k] * image[...])
+        second = send_back(acc, par)
+        around = forward_own(w, own_part(acc))
+        for cp in first:
+            cp.wait()
+        around = forward_ghosts(par, around)
         dots = take_dots(third, par)
         light = dots[3]
         alpha, beta, state = step_sizes(dots, state, start)
-        r, w = residual[...], image[...]
+        q = degree[...] * w - 0.5 * (around + take_back(second, par))
         z = q + beta * image2[...]
         s = w + beta * steps[...]
         p = r + beta * direction[...]
@@ -659,44 +766,44 @@
     zero = jnp.zeros((8, 1), F32)
     state = lax.fori_loop(0, ITERS - 1, sweep, (zero + 1.0, zero, zero, zero))
     par = ITERS % 2
-    dots = take_dots(send_dots(par), par)
+    parts[par, me] = dots_of(residual[...])
+    third = send_dots(par, others)
+    first_layer[...] = product(last1[...], features_of(feat_ref))
+    dots = take_dots(third, par)
     alpha, beta, state = step_sizes(dots, state, False)
     x = total[...] + alpha * (residual[...] + beta * direction[...])
     sums = state[3]
-    charge_ref[...] = x[0:PER] - (sums[0:PER] / sums[PER:8]) * x[PER:8]
-
-
-def energies_kernel(
-    feat_ref,
-    charge_ref,
-    newpos_ref,
-    newmom_ref,
-    types_ref,
-    w1_ref,
-    w2_ref,
-    w3_ref,
-    pos_out,
-    mom_out,
-    charge_out,
-    out_ref,
-    full,
-    wide1,
-    wide2,
-    wide3,
-):
-    pos_out[...] = newpos_ref[...]
-    mom_out[...] = newmom_ref[...]
-    charge_out[...] = charge_ref[...]
-    load_weights(w1_ref, w2_ref, w3_ref, wide1, wide2, wide3)
-    full[...] = feat_ref[...]
-    for d in range(CHUNKS):
-        full[d, FEATS * PER : (FEATS + 1) * PER, :] = charge_ref[:, d * LANES : (d + 1) * LANES]
-    for b, e in enumerate(network(full, wide1, wide2, wide3, types_ref[...] == 0)):
-        out_ref[b : b + 1, :] = e
+    charges = x[0:PER] - (sums[0:PER] / sums[PER:8]) * x[PER:8]
+    charge_ref[...] = charges
+    storing.append(pltpu.make_async_copy(charge_ref, charge_hbm, stores.at[2]))
+    storing[2].start()
+    column = last1[:, FEATS : FEATS + 1]
+    hidden = jnp.concatenate(
+        [
+            first_layer[:, b * ATOMS : (b + 1) * ATOMS] + column * charges[b : b + 1]
+            for b in range(PER)
+        ],
+        1,
+    )
+    for b, e in enumerate(network(hidden, last2, last3, heavy_row)):
+        energy_ref[b : b + 1, :] = e
+    storing.append(pltpu.make_async_copy(energy_ref, energy_hbm, stores.at[3]))
+    storing[3].start()
+    for cp in storing:
+        cp.wait()
+
+
+def outputs_kernel(a_ref, b_ref, c_ref, d_ref, a_out, b_out, c_out, d_out):
+    for src, dst in ((a_ref, a_out), (b_ref, b_out), (c_ref, c_out), (d_ref, d_out)):
+        dst[...] = src[...]
 
 
 def vmem(count):
     return [pl.BlockSpec(memory_space=pltpu.VMEM)] * count
+
+
+def anywhere(count):
+    return [pl.BlockSpec(memory_space=pl.ANY)] * count
 
 
 def sds(*shape, dtype=F32):
@@ -722,25 +829,37 @@
     en_w2,
     en_w3,
 ):
-    types = types.reshape(1, ATOMS)
-    counts = counts.reshape(1, ATOMS)
-    ghost_rows = ghost_rows.reshape(1, LANES)
     turn = lambda v: jnp.transpose(v, (1, 0, 2))
     dma = pltpu.SemaphoreType.DMA
-    i32 = jnp.int32
     networks = [f32(2 * PAD, PAD), f32(2 * PAD, 2 * PAD), f32(8, 2 * PAD)]
-    new_pos, new_mom, charges, feats = pl.pallas_call(
+    operands = (
+        hardness,
+        jnp.asarray(propagator()),
+        turn(positions),
+        turn(momenta),
+        types.reshape(1, ATOMS),
+        ghost_rows.reshape(1, LANES),
+        neighbours,
+        counts.reshape(1, ATOMS),
+        turn(chi_w1),
+        turn(chi_w2),
+        chi_w3,
+        turn(en_w1),
+        turn(en_w2),
+        en_w3,
+    )
+    outputs = (sds(3, PER, ATOMS), sds(3, PER, ATOMS), sds(PER, ATOMS), sds(PER, ATOMS))
+    results = pl.pallas_call(
         main_kernel,
         name="main",
-        out_shape=(
-            sds(3, PER, ATOMS),
-            sds(3, PER, ATOMS),
-            sds(PER, ATOMS),
-            sds(CHUNKS, LANES, LANES),
-        ),
-        in_specs=[pl.BlockSpec(memory_space=pltpu.SMEM)] + vmem(10),
-        out_specs=tuple(vmem(4)),
+        out_shape=outputs,
+        in_specs=anywhere(len(operands)),
+        out_specs=tuple(anywhere(len(outputs))),
         scratch_shapes=[
+            pltpu.SMEM(hardness.shape, F32),
+            *[pltpu.VMEM(v.shape, v.dtype) for v in operands[1:]],
+            *[f32(*v.shape) for v in outputs],
+            f32(CHUNKS, LANES, LANES),
             f32(8, 6 * ATOMS),
             f32(64, 6 * LANES),
             f32(64, 3 * LANES),
@@ -748,58 +867,47 @@
             f32(3, 8, LANES),
             f32(8, LANES),
             f32(4, 8, TABLE),
-            pltpu.VMEM((SLOTS, ATOMS), i32),
+            pltpu.VMEM((SLOTS, ATOMS), jnp.int32),
             f32(SLOTS, ATOMS),
-            pltpu.VMEM((SLOTS, 8, ATOMS), i32),
-            pltpu.VMEM((SLOTS // 2, 8, ATOMS), i32),
+            pltpu.VMEM((SLOTS, 8, ATOMS), jnp.int32),
+            pltpu.VMEM((SLOTS // 2, 8, ATOMS), jnp.int32),
             f32(SLOTS // 2, 8, ATOMS),
             pltpu.VMEM((SLOTS, BAND, ATOMS), BF16),
             pltpu.VMEM((WIDE, EDGES), BF16),
             pltpu.VMEM((EDGES, WIDE), BF16),
-            pltpu.VMEM((ATOMS, LANES), BF16),
-            f32(SLOTS, 8, ATOMS),
-            f32(SLOTS, 8, ATOMS),
+            pltpu.VMEM((LANES, ATOMS), BF16),
             f32(SLOTS, 8, ATOMS),
             f32(SLOTS // 2, 8, ATOMS),
             f32(SLOTS // 2, 8, ATOMS),
             f32(SLOTS // 2, 8, ATOMS),
             *networks,
+            *networks,
+            f32(2 * PAD, PER * ATOMS),
             *[f32(8, ATOMS) for _ in range(7)],
-            f32(2, 8, ATOMS),
-            f32(2, 8, 8, LANES),
+            f32(3, 8, 8, LANES),
             f32(2, 8, LANES),
             f32(2, 8, 8, LANES),
+            f32(3, 8, 8, LANES),
             f32(2, BRICKS, 8, LANES),
             *[dma((GROUPS,)) for _ in range(4)],
             *[dma((8,)) for _ in range(4)],
-            *[dma((2, 8)) for _ in range(4)],
+            *[dma((2, 8)) for _ in range(2)],
+            *[dma((3, 8)) for _ in range(2)],
             *[dma((2, BRICKS)) for _ in range(2)],
+            dma((len(operands),)),
+            dma((len(outputs),)),
         ],
         compiler_params=pltpu.CompilerParams(
             vmem_limit_bytes=VMEM_LIMIT, collective_id=0, has_side_effects=True
         ),
-    )(
-        hardness,
-        jnp.asarray(propagator()),
-        turn(positions),
-        turn(momenta),
-        types,
-        ghost_rows,
-        neighbours,
-        counts,
-        turn(chi_w1),
-        turn(chi_w2),
-        chi_w3,
-    )
+    )(*operands)
     new_pos, new_mom, charges, energies = pl.pallas_call(
-        energies_kernel,
-        name="energies",
-        out_shape=(sds(3, PER, ATOMS), sds(3, PER, ATOMS), sds(PER, ATOMS), sds(PER, ATOMS)),
-        in_specs=vmem(8),
-        out_specs=tuple(vmem(4)),
-        scratch_shapes=[f32(CHUNKS, LANES, LANES), *networks],
-        compiler_params=pltpu.CompilerParams(vmem_limit_bytes=VMEM_LIMIT),
-    )(feats, charges, new_pos, new_mom, types, turn(en_w1), turn(en_w2), en_w3)
+        outputs_kernel,
+        name="outputs",
+        out_shape=outputs,
+        in_specs=vmem(len(outputs)),
+        out_specs=tuple(vmem(len(outputs))),
+    )(*results)
     return (turn(new_pos), turn(new_mom), charges, energies)
 
 

time: 78.1 us -> 73.4 us (0.940)
  Pallas kernels: 77.3 us -> 72.5 us
    pallas_call x2, Pallas kernels: 77.3 us -> 72.5 us  [the longest x1 71 us: on_device(): pl.pallas_call(main_kernel, name='main', out_shape=outputs, in_specs=anyw...]
where the time goes in v3:
time: 73.4 us; the launch traced here: 73.2 us
  Pallas kernels  72.5 us (99%)
    pallas_call x1, Pallas kernels, on_device(): pl.pallas_call(main_kernel, name='main', out_shape=outputs, in_specs=anyw...  71 us
    pallas_call x1, Pallas kernels, on_device(): pl.pallas_call(outputs_kernel, name='outputs', out_shape=outputs, in_spec...  1.48 us

profile of v3, /device:TPU:0, one launch (start us, length us, event | category | flops | bytes accessed | tf_op | source)
XLA Modules:
  0.0 73.2 jit_solution(2675340776626106417)
XLA Ops:
  0.6 71.0 %main.1 = (f32[3,4,1024]{2,1,0:T(4,128)}, f32[3,4,1024]{2,1,0:T(4,128)}, f32[4,1024]{1,0:T(4,128)}, f32[4,1024]{1,0:T(4,128)}) custom-call(f32[2]{0:T(128)} %hardness_hbm.1, f32[128,64]{1,0:T(8,128)} %constant.2.clone.matrix_hbm, f32[3,4,1024]{2,1,0:T(4,128)} %bitcast.11, f32[3,4,1024]{2,1,0:T(4,128)} %bitcast.12, s32[1,1024]{1,0:T(1,128)} %bitcast.17, ...), custom_call_target="tpu_custom_call" | custom-call | tf_op jit(solution)/shard_map/main/pallas_call | solution.py:852
  71.7 1.5 %outputs.1 = (f32[3,4,1024]{2,1,0:T(4,128)}, f32[3,4,1024]{2,1,0:T(4,128)}, f32[4,1024]{1,0:T(4,128)}, f32[4,1024]{1,0:T(4,128)}) custom-call(f32[3,4,1024]{2,1,0:T(4,128)} %get-tuple-element.12.a_ref, f32[3,4,1024]{2,1,0:T(4,128)} %get-tuple-element.13.b_ref, f32[4,1024]{1,0:T(4,128)} %get-tuple-element.14.c_ref, f32[4,1024]{1,0:T(4,128)} %get-tuple-element.15.d_ref), custom_call_target="tpu_custom_call" | custom-call | tf_op jit(solution)/shard_map/outputs/pallas_call | solution.py:904

commit v4 on v3

--- a/solution.py
+++ b/solution.py
@@ -145,8 +145,7 @@
 
 
 def network(hidden, wide2, wide3, heavy):
-    h = jnp.tanh(product(wide2[...], jnp.tanh(hidden)))
-    out = product(wide3[...], h)
+    out = product(wide3[...], jnp.tanh(product(wide2[...], jnp.tanh(hidden))))
     return [
         jnp.where(
             heavy, out[0:1, b * ATOMS : (b + 1) * ATOMS], out[1:2, b * ATOMS : (b + 1) * ATOMS]
@@ -252,6 +251,7 @@
     group = lax.axis_index("bead")
     me = lax.axis_index("gx") * SIDE + lax.axis_index("gy")
     others = [(o // SIDE, o % SIDE) for o in range(1, BRICKS)]
+    parts[...] = jnp.zeros_like(parts)
     barrier = pltpu.get_barrier_semaphore()
     for o in range(1, GROUPS):
         pl.semaphore_signal(
@@ -345,27 +345,44 @@
 
     for cp in loading[4:]:
         cp.wait()
-    for half in range(2):
-        for d in range(CHUNKS):
-            lanes = slice(d * LANES, (d + 1) * LANES)
+    def renumber(d, carry):
+        lanes = pl.ds(pl.multiple_of(d * LANES, LANES), LANES)
+        for half in range(2):
             rows = idx_ref[half * 8 : half * 8 + 8, lanes]
             local = lane_take(ghost_rows, rows & (LANES - 1))
             rows = jnp.where(
                 rows < SELF, rows, jnp.where(rows < SELF + LANES, local, rows - LANES)
             )
             idx16[half * 8 : half * 8 + 8, lanes] = rows
+        return carry
+
+    lax.fori_loop(0, CHUNKS, renumber, 0)
     for k in range(SLOTS):
         rows_all[k] = jnp.broadcast_to(idx16[k : k + 1, :], (8, ATOMS))
-        block_ids[k] = jnp.broadcast_to(
-            (idx16[k : k + 1, :] >> 8).astype(F32), (BAND, ATOMS)
-        ).astype(BF16)
-    for kp in range(SLOTS // 2):
+    within = sublanes((WIDE, ATOMS)).astype(F32).astype(BF16)
+
+    def build(k, carry):
+        rows = rows_all[k]
+        ids = (rows >> 8).astype(F32)
+        block_ids[k] = jnp.concatenate([ids, ids], 0).astype(BF16)
+        wide = (rows & (WIDE - 1)).astype(F32)
+        wide = jnp.concatenate([wide, wide], 0).astype(BF16)
+        wide = jnp.concatenate([wide] * (WIDE // BAND), 0)
+        edges = pl.ds(pl.multiple_of(k * ATOMS, ATOMS), ATOMS)
+        hits = jnp.where(within == wide, 1.0, 0.0).astype(BF16)
+        onehot[:, edges] = hits
+        onehot_t[edges, :] = jnp.transpose(hits)
+        return carry
+
+    lax.fori_loop(0, SLOTS, build, 0)
+    for ref in (coup, dist, weight_h, weight_l, feat_ref):
+        ref[...] = jnp.zeros_like(ref)
+
+    def pair_up(kp, carry):
         pairs[kp] = jnp.where(low_all, rows_all[2 * kp], rows_all[2 * kp + 1])
-    within = sublanes((WIDE, ATOMS)).astype(F32).astype(BF16)
-    for k in range(SLOTS):
-        wide = jnp.broadcast_to((idx16[k : k + 1, :] & (WIDE - 1)).astype(F32), (BAND, ATOMS))
-        wide = jnp.concatenate([wide.astype(BF16)] * (WIDE // BAND), 0)
-        onehot[:, k * ATOMS : (k + 1) * ATOMS] = jnp.where(within == wide, 1.0, 0.0).astype(BF16)
+        return carry
+
+    lax.fori_loop(0, SLOTS // 2, pair_up, 0)
     load_weights(w1_ref, w2_ref, w3_ref, wide1, wide2, wide3)
     load_weights(v1_ref, v2_ref, v3_ref, last1, last2, last3)
     my_types = types_ref[:, pl.ds(pl.multiple_of(group * LANES, LANES), LANES)]
@@ -418,16 +435,20 @@
         copies.append(cp)
     back[:, my_lanes] = moved[mine, :]
 
-    for d in range(CHUNKS):
+    def ghost_hits(d, carry):
         rows = sublanes((LANES, LANES)) + d * LANES
         hit = rows == jnp.broadcast_to(ghost_ref[...], (LANES, LANES))
         hit = jnp.where(hit, 1.0, 0.0).astype(BF16)
-        ghost_onehot[:, d * LANES : (d + 1) * LANES] = jnp.transpose(hit)
+        ghost_onehot[:, pl.ds(pl.multiple_of(d * LANES, LANES), LANES)] = jnp.transpose(hit)
+        return carry
+
+    lax.fori_loop(0, CHUNKS, ghost_hits, 0)
     for cp in heavy_copies:
         cp.wait()
-    for half in range(2):
-        for d in range(CHUNKS):
-            lanes = slice(d * LANES, (d + 1) * LANES)
+
+    def near_heavy(d, carry):
+        lanes = pl.ds(pl.multiple_of(d * LANES, LANES), LANES)
+        for half in range(2):
             rows = idx16[half * 8 : half * 8 + 8, lanes]
             lane = rows & (LANES - 1)
             heavy16[half * 8 : half * 8 + 8, lanes] = pick(
@@ -437,16 +458,16 @@
                 ],
                 row_bits(rows, 4),
             )
+        return carry
+
+    lax.fori_loop(0, CHUNKS, near_heavy, 0)
     for kp in range(SLOTS // 2):
         heavy_pairs[kp] = jnp.where(
             low_all,
             jnp.broadcast_to(heavy16[2 * kp : 2 * kp + 1, :], (8, ATOMS)),
             jnp.broadcast_to(heavy16[2 * kp + 1 : 2 * kp + 2, :], (8, ATOMS)),
         )
-    for k in range(SLOTS):
-        onehot_t[k * ATOMS : (k + 1) * ATOMS, :] = jnp.transpose(
-            onehot[:, k * ATOMS : (k + 1) * ATOMS]
-        )
+
 
     for cp in copies:
         cp.wait()
@@ -470,7 +491,45 @@
     cos_scale = (math.pi / (2.0 * CUTOFF)) ** 2
     cos_terms = [(-1.0) ** n * cos_scale**n / math.factorial(2 * n) for n in range(8)]
 
-    def geometry(ci, carry):
+    def by_block(terms, ids):
+        terms = split(terms)
+        zero = jnp.zeros_like(terms)
+        return jnp.concatenate([jnp.where(ids == b, terms, zero) for b in range(BLOCKS)], 0)
+
+    def radial(ci):
+        lanes = pl.ds(pl.multiple_of(ci * LANES, LANES), LANES)
+        sums = [jnp.zeros((8, LANES), F32) for _ in range(FEATS)]
+        for kp in range(SLOTS // 2):
+            d = dist[kp, :, lanes]
+            wh = weight_h[kp, :, lanes]
+            wl = weight_l[kp, :, lanes]
+            for s in range(HALF):
+                rate = -0.2 * 20.0 ** (s / (HALF - 1)) * math.log2(math.e)
+                falloff = jnp.exp2(d * rate)
+                sums[s] = sums[s] + wh * falloff
+                sums[HALF + s] = sums[HALF + s] + wl * falloff
+        for s in range(FEATS):
+            v = jnp.log(1.0 + (sums[s] + pltpu.roll(sums[s], PER, 0)))
+            feat_ref[ci, s * PER : (s + 1) * PER, :] = v[0:PER]
+
+    def degree_part(ci, acc):
+        lanes = pl.ds(pl.multiple_of(ci * LANES, LANES), LANES)
+        tall = jnp.concatenate(
+            [by_block(coup[k, :, lanes], block_ids[k, :, lanes]) for k in range(SLOTS)], 1
+        )
+        hits = jnp.concatenate(
+            [
+                onehot_t[pl.ds(pl.multiple_of(k * ATOMS + ci * LANES, LANES), LANES), :]
+                for k in range(SLOTS)
+            ],
+            0,
+        )
+        return acc + jnp.dot(tall, hits, preferred_element_type=F32)
+
+    def geometry(ci, acc):
+        before = lax.rem(ci + CHUNKS - 1, CHUNKS)
+        acc = degree_part(before, acc)
+        radial(before)
         lanes = pl.ds(pl.multiple_of(ci * LANES, LANES), LANES)
         own = [tab[c, :, lanes] for c in range(3)]
         count = jnp.broadcast_to(counts_ref[:, lanes], (8, LANES))
@@ -502,27 +561,18 @@
             turned = pltpu.roll(coupling, PER, 0)
             for k, v in ((2 * kp, jnp.where(low, coupling, turned)), (2 * kp + 1, jnp.where(low, turned, coupling))):
                 coup[k, :, lanes] = v
-        return carry
-
-    lax.fori_loop(0, CHUNKS, geometry, 0)
-
-    def scatter(terms_of, beside=None):
+        return acc
+
+    acc = lax.fori_loop(0, CHUNKS, geometry, jnp.zeros((BLOCKS * BAND, WIDE), F32))
+    acc = degree_part(CHUNKS - 1, acc)
+
+    def scatter(terms_of):
         acc = jnp.zeros((BLOCKS * BAND, WIDE), F32)
         for g in range(SLOTS // GROUP):
-            if beside is not None:
-                beside(g)
-            tall = []
-            for k in range(g * GROUP, (g + 1) * GROUP):
-                terms = split(terms_of(k))
-                zero = jnp.zeros_like(terms)
-                ids = block_ids[k]
-                tall.append(
-                    jnp.concatenate([jnp.where(ids == b, terms, zero) for b in range(BLOCKS)], 0)
-                )
+            group_slots = range(g * GROUP, (g + 1) * GROUP)
+            tall = jnp.concatenate([by_block(terms_of(k), block_ids[k]) for k in group_slots], 1)
             rows = slice(g * GROUP * ATOMS, (g + 1) * GROUP * ATOMS)
-            acc = acc + jnp.dot(
-                jnp.concatenate(tall, 1), onehot_t[rows, :], preferred_element_type=F32
-            )
+            acc = acc + jnp.dot(tall, onehot_t[rows, :], preferred_element_type=F32)
         return acc
 
     def chunk_of(acc, n):
@@ -609,30 +659,8 @@
             acc = by_lookup(chunks, half + g, acc)
         return acc
 
-    feat_ref[...] = jnp.zeros_like(feat_ref)
-
-    def radial(ci):
-        lanes = slice(ci * LANES, (ci + 1) * LANES)
-        sums = [jnp.zeros((8, LANES), F32) for _ in range(FEATS)]
-        for kp in range(SLOTS // 2):
-            d = dist[kp, :, lanes]
-            wh = weight_h[kp, :, lanes]
-            wl = weight_l[kp, :, lanes]
-            for s in range(HALF):
-                rate = -0.2 * 20.0 ** (s / (HALF - 1)) * math.log2(math.e)
-                falloff = jnp.exp2(d * rate)
-                sums[s] = sums[s] + wh * falloff
-                sums[HALF + s] = sums[HALF + s] + wl * falloff
-        for s in range(FEATS):
-            v = jnp.log(1.0 + (sums[s] + pltpu.roll(sums[s], PER, 0)))
-            feat_ref[ci, s * PER : (s + 1) * PER, :] = v[0:PER]
-
-    def radial_pair(g):
-        radial(2 * g)
-        radial(2 * g + 1)
-
-    acc = scatter(lambda k: coup[k], radial_pair)
     first_back = send_back(acc, 2)
+    radial(CHUNKS - 1)
     around = own_part(acc)
     for k in range(SLOTS):
         around = around + coup[k]
@@ -670,20 +698,26 @@
             out.append(cp)
         return out
 
-    def send_dots(par, targets):
+    def dot_copies(par, targets):
         out = []
         for dx, dy in targets:
             n = dx * SIDE + dy
-            cp = pltpu.make_async_remote_copy(
-                src_ref=parts.at[par, me],
-                dst_ref=parts.at[par, me],
-                send_sem=send_d.at[par, n],
-                recv_sem=recv_d.at[par, n],
-                device_id=brick_at(dx, dy),
-                device_id_type=MESH,
+            out.append(
+                pltpu.make_async_remote_copy(
+                    src_ref=parts.at[par, me],
+                    dst_ref=parts.at[par, me],
+                    send_sem=send_d.at[par, n],
+                    recv_sem=recv_d.at[par, n],
+                    device_id=brick_at(dx, dy),
+                    device_id_type=MESH,
+                )
             )
+        return out
+
+    def send_dots(par, targets):
+        out = dot_copies(par, targets)
+        for cp in out:
             cp.start()
-            out.append(cp)
         return out
 
     def take_dots(copies, par):
@@ -705,35 +739,40 @@
         p_sum = r_sum + beta * sum_prev
         return alpha, beta, (norm, curve, p_sum, sum_total + alpha * p_sum)
 
-    copies = send_lent(residual, 0)
-    acc = scatter(lambda k: coup[k] * residual[...])
-    second = send_back(acc, 0)
-    around = forward_own(residual[...], own_part(acc))
-    deg = hard + 0.5 * (degree[...] + take_back(first_back, 2))
-    degree[...] = deg
-    for cp in copies:
-        cp.wait()
-    around = forward_ghosts(0, around)
-    image[...] = deg * residual[...] - 0.5 * (around + take_back(second, 0))
+    image[...] = residual[...]
     for ref in (direction, steps, image2, total):
         ref[...] = jnp.zeros_like(ref)
     high = jnp.logical_not(low_all)
     high_col = sublanes((8, 1)) >= PER
 
     def sweep(it, state):
-        par = lax.rem(it + 1, 2)
-        start = it == 0
+        par = lax.rem(it, 2)
+        start = it == 1
         r, w = residual[...], image[...]
         first = send_lent(image, par)
-        parts[par, me] = dots_of(r)
-        third = send_dots(par, others)
+
+        @pl.when(it > 0)
+        def _():
+            parts[par, me] = dots_of(r)
+            send_dots(par, others)
+
         acc = scatter(lambda k: coup[k] * image[...])
         second = send_back(acc, par)
         around = forward_own(w, own_part(acc))
         for cp in first:
             cp.wait()
         around = forward_ghosts(par, around)
-        dots = take_dots(third, par)
+
+        @pl.when(it == 0)
+        def _():
+            degree[...] = hard + 0.5 * (degree[...] + take_back(first_back, 2))
+
+        @pl.when(it > 0)
+        def _():
+            for cp in dot_copies(par, others):
+                cp.wait()
+
+        dots = take_dots([], par)
         light = dots[3]
         alpha, beta, state = step_sizes(dots, state, start)
         q = degree[...] * w - 0.5 * (around + take_back(second, par))
@@ -753,7 +792,7 @@
         image2[...] = jnp.where(known, h0 * hard + gap * w, z)
         total[...] = jnp.where(known, TOTAL_ATOMS / hard_sum, x)
         residual[...] = jnp.where(known, gap * (c0 + c1 * r), r_new)
-        image[...] = jnp.where(known, gap * (c0 * hard + c1 * w), w_new)
+        image[...] = jnp.where(it == 0, q, jnp.where(known, gap * (c0 * hard + c1 * w), w_new))
         exact = (
             jnp.full((8, 1), TOTAL_ATOMS, F32),
             hard_sum,
@@ -764,10 +803,11 @@
         return tuple(jnp.where(known_col, e, v) for e, v in zip(exact, state))
 
     zero = jnp.zeros((8, 1), F32)
-    state = lax.fori_loop(0, ITERS - 1, sweep, (zero + 1.0, zero, zero, zero))
+    state = lax.fori_loop(0, ITERS, sweep, (zero, zero, zero, zero))
     par = ITERS % 2
     parts[par, me] = dots_of(residual[...])
     third = send_dots(par, others)
+
     first_layer[...] = product(last1[...], features_of(feat_ref))
     dots = take_dots(third, par)
     alpha, beta, state = step_sizes(dots, state, False)
@@ -778,6 +818,7 @@
     storing.append(pltpu.make_async_copy(charge_ref, charge_hbm, stores.at[2]))
     storing[2].start()
     column = last1[:, FEATS : FEATS + 1]
+
     hidden = jnp.concatenate(
         [
             first_layer[:, b * ATOMS : (b + 1) * ATOMS] + column * charges[b : b + 1]

time: 73.4 us -> 69.6 us (0.948)
  Pallas kernels: 72.5 us -> 68.7 us
    pallas_call x1, Pallas kernels: 71 us -> 67.2 us  [on_device(): pl.pallas_call(main_kernel, name='main', out_shape=outputs, in_specs=anyw...]
where the time goes in v4:
time: 69.6 us; the launch traced here: 69.3 us
  Pallas kernels  68.7 us (99%)
    pallas_call x1, Pallas kernels, on_device(): pl.pallas_call(main_kernel, name='main', out_shape=outputs, in_specs=anyw...  67.2 us
    pallas_call x1, Pallas kernels, on_device(): pl.pallas_call(outputs_kernel, name='outputs', out_shape=outputs, in_spec...  1.48 us

profile of v4, /device:TPU:0, one launch (start us, length us, event | category | flops | bytes accessed | tf_op | source)
XLA Modules:
  0.0 69.3 jit_solution(9510755035120820979)
XLA Ops:
  0.6 67.2 %main.1 = (f32[3,4,1024]{2,1,0:T(4,128)}, f32[3,4,1024]{2,1,0:T(4,128)}, f32[4,1024]{1,0:T(4,128)}, f32[4,1024]{1,0:T(4,128)}) custom-call(f32[2]{0:T(128)} %hardness_hbm.1, f32[128,64]{1,0:T(8,128)} %constant.2.clone.matrix_hbm, f32[3,4,1024]{2,1,0:T(4,128)} %bitcast.11, f32[3,4,1024]{2,1,0:T(4,128)} %bitcast.12, s32[1,1024]{1,0:T(1,128)} %bitcast.17, ...), custom_call_target="tpu_custom_call" | custom-call | tf_op jit(solution)/shard_map/main/pallas_call | solution.py:893
  67.9 1.5 %outputs.1 = (f32[3,4,1024]{2,1,0:T(4,128)}, f32[3,4,1024]{2,1,0:T(4,128)}, f32[4,1024]{1,0:T(4,128)}, f32[4,1024]{1,0:T(4,128)}) custom-call(f32[3,4,1024]{2,1,0:T(4,128)} %get-tuple-element.12.a_ref, f32[3,4,1024]{2,1,0:T(4,128)} %get-tuple-element.13.b_ref, f32[4,1024]{1,0:T(4,128)} %get-tuple-element.14.c_ref, f32[4,1024]{1,0:T(4,128)} %get-tuple-element.15.d_ref), custom_call_target="tpu_custom_call" | custom-call | tf_op jit(solution)/shard_map/outputs/pallas_call | solution.py:945

commit v5 on v4

--- a/solution.py
+++ b/solution.py
@@ -38,6 +38,7 @@
 OWN_BLOCKS = ATOMS // WIDE
 EDGES = SLOTS * ATOMS
 GROUP = 4
+EARLY = 10
 TOTAL_ATOMS = ATOMS * BRICKS
 TINY = 1e-30
 SELF = ATOMS + 4 * LANES
@@ -374,7 +375,7 @@
         onehot_t[edges, :] = jnp.transpose(hits)
         return carry
 
-    lax.fori_loop(0, SLOTS, build, 0)
+    lax.fori_loop(0, EARLY, build, 0)
     for ref in (coup, dist, weight_h, weight_l, feat_ref):
         ref[...] = jnp.zeros_like(ref)
 
@@ -461,6 +462,7 @@
         return carry
 
     lax.fori_loop(0, CHUNKS, near_heavy, 0)
+    lax.fori_loop(EARLY, SLOTS, build, 0)
     for kp in range(SLOTS // 2):
         heavy_pairs[kp] = jnp.where(
             low_all,
@@ -566,9 +568,10 @@
     acc = lax.fori_loop(0, CHUNKS, geometry, jnp.zeros((BLOCKS * BAND, WIDE), F32))
     acc = degree_part(CHUNKS - 1, acc)
 
-    def scatter(terms_of):
+    def scatter(terms_of, beside):
         acc = jnp.zeros((BLOCKS * BAND, WIDE), F32)
         for g in range(SLOTS // GROUP):
+            beside(g)
             group_slots = range(g * GROUP, (g + 1) * GROUP)
             tall = jnp.concatenate([by_block(terms_of(k), block_ids[k]) for k in group_slots], 1)
             rows = slice(g * GROUP * ATOMS, (g + 1) * GROUP * ATOMS)
@@ -750,13 +753,14 @@
         start = it == 1
         r, w = residual[...], image[...]
         first = send_lent(image, par)
-
-        @pl.when(it > 0)
-        def _():
-            parts[par, me] = dots_of(r)
-            send_dots(par, others)
-
-        acc = scatter(lambda k: coup[k] * image[...])
+        third = []
+
+        def dots_beside(g):
+            if g == 2:
+                parts[par, me] = dots_of(r)
+                third.extend(send_dots(par, others))
+
+        acc = scatter(lambda k: coup[k] * image[...], dots_beside)
         second = send_back(acc, par)
         around = forward_own(w, own_part(acc))
         for cp in first:
@@ -766,15 +770,11 @@
         @pl.when(it == 0)
         def _():
             degree[...] = hard + 0.5 * (degree[...] + take_back(first_back, 2))
-
-        @pl.when(it > 0)
-        def _():
-            for cp in dot_copies(par, others):
-                cp.wait()
-
-        dots = take_dots([], par)
+        dots = take_dots(third, par)
         light = dots[3]
-        alpha, beta, state = step_sizes(dots, state, start)
+        alpha, beta, state = step_sizes(dots, state, it <= 1)
+        alpha = jnp.where(it == 0, 0.0, alpha)
+        state = tuple(jnp.where(it == 0, 0.0, v) for v in state)
         q = degree[...] * w - 0.5 * (around + take_back(second, par))
         z = q + beta * image2[...]
         s = w + beta * steps[...]

time: 69.6 us -> 67.9 us (0.976)
  Pallas kernels: 68.7 us -> 67.1 us
    pallas_call x1, Pallas kernels: 67.2 us -> 65.6 us  [on_device(): pl.pallas_call(main_kernel, name='main', out_shape=outputs, in_specs=anyw...]
where the time goes in v5:
time: 67.9 us; the launch traced here: 67.7 us
  Pallas kernels  67.1 us (99%)
    pallas_call x1, Pallas kernels, on_device(): pl.pallas_call(main_kernel, name='main', out_shape=outputs, in_specs=anyw...  65.6 us
    pallas_call x1, Pallas kernels, on_device(): pl.pallas_call(outputs_kernel, name='outputs', out_shape=outputs, in_spec...  1.48 us

profile of v5, /device:TPU:0, one launch (start us, length us, event | category | flops | bytes accessed | tf_op | source)
XLA Modules:
  0.0 67.7 jit_solution(3814346928229086556)
XLA Ops:
  0.6 65.6 %main.1 = (f32[3,4,1024]{2,1,0:T(4,128)}, f32[3,4,1024]{2,1,0:T(4,128)}, f32[4,1024]{1,0:T(4,128)}, f32[4,1024]{1,0:T(4,128)}) custom-call(f32[2]{0:T(128)} %hardness_hbm.1, f32[128,64]{1,0:T(8,128)} %constant.2.clone.matrix_hbm, f32[3,4,1024]{2,1,0:T(4,128)} %bitcast.11, f32[3,4,1024]{2,1,0:T(4,128)} %bitcast.12, s32[1,1024]{1,0:T(1,128)} %bitcast.17, ...), custom_call_target="tpu_custom_call" | custom-call | tf_op jit(solution)/shard_map/main/pallas_call | solution.py:893
  66.3 1.5 %outputs.1 = (f32[3,4,1024]{2,1,0:T(4,128)}, f32[3,4,1024]{2,1,0:T(4,128)}, f32[4,1024]{1,0:T(4,128)}, f32[4,1024]{1,0:T(4,128)}) custom-call(f32[3,4,1024]{2,1,0:T(4,128)} %get-tuple-element.12.a_ref, f32[3,4,1024]{2,1,0:T(4,128)} %get-tuple-element.13.b_ref, f32[4,1024]{1,0:T(4,128)} %get-tuple-element.14.c_ref, f32[4,1024]{1,0:T(4,128)} %get-tuple-element.15.d_ref), custom_call_target="tpu_custom_call" | custom-call | tf_op jit(solution)/shard_map/outputs/pallas_call | solution.py:945

commit v6 on v5

--- a/solution.py
+++ b/solution.py
@@ -763,13 +763,15 @@
         acc = scatter(lambda k: coup[k] * image[...], dots_beside)
         second = send_back(acc, par)
         around = forward_own(w, own_part(acc))
+
+        @pl.when(it == 0)
+        def _():
+            degree[...] = hard + 0.5 * (degree[...] + take_back(first_back, 2))
+
         for cp in first:
             cp.wait()
         around = forward_ghosts(par, around)
 
-        @pl.when(it == 0)
-        def _():
-            degree[...] = hard + 0.5 * (degree[...] + take_back(first_back, 2))
         dots = take_dots(third, par)
         light = dots[3]
         alpha, beta, state = step_sizes(dots, state, it <= 1)

time: 67.9 us -> 68 us (level)
  no operation moved by 1% of the time
where the time goes in v6:
time: 68 us; the launch traced here: 67.8 us
  Pallas kernels  67.1 us (99%)
    pallas_call x1, Pallas kernels, on_device(): pl.pallas_call(main_kernel, name='main', out_shape=outputs, in_specs=anyw...  65.6 us
    pallas_call x1, Pallas kernels, on_device(): pl.pallas_call(outputs_kernel, name='outputs', out_shape=outputs, in_spec...  1.48 us

profile of v6, /device:TPU:0, one launch (start us, length us, event | category | flops | bytes accessed | tf_op | source)
XLA Modules:
  0.0 67.8 jit_solution(12316472773115208967)
XLA Ops:
  0.6 65.6 %main.1 = (f32[3,4,1024]{2,1,0:T(4,128)}, f32[3,4,1024]{2,1,0:T(4,128)}, f32[4,1024]{1,0:T(4,128)}, f32[4,1024]{1,0:T(4,128)}) custom-call(f32[2]{0:T(128)} %hardness_hbm.1, f32[128,64]{1,0:T(8,128)} %constant.2.clone.matrix_hbm, f32[3,4,1024]{2,1,0:T(4,128)} %bitcast.11, f32[3,4,1024]{2,1,0:T(4,128)} %bitcast.12, s32[1,1024]{1,0:T(1,128)} %bitcast.17, ...), custom_call_target="tpu_custom_call" | custom-call | tf_op jit(solution)/shard_map/main/pallas_call | solution.py:895
  66.3 1.5 %outputs.1 = (f32[3,4,1024]{2,1,0:T(4,128)}, f32[3,4,1024]{2,1,0:T(4,128)}, f32[4,1024]{1,0:T(4,128)}, f32[4,1024]{1,0:T(4,128)}) custom-call(f32[3,4,1024]{2,1,0:T(4,128)} %get-tuple-element.12.a_ref, f32[3,4,1024]{2,1,0:T(4,128)} %get-tuple-element.13.b_ref, f32[4,1024]{1,0:T(4,128)} %get-tuple-element.14.c_ref, f32[4,1024]{1,0:T(4,128)} %get-tuple-element.15.d_ref), custom_call_target="tpu_custom_call" | custom-call | tf_op jit(solution)/shard_map/outputs/pallas_call | solution.py:947
